TPU v7x, 512 devices: a whole 4x8x8 slice. The times are simulated.
512 devices in a mesh: scen: 8 (over x, core), reach: 64 (over y, z).
Axes of the slice: x: 4, y: 8, z: 8, core: 2. Of those that a mesh axis runs over, the one named last changes fastest.
Arguments:
- perturb: float32 [8, 2, 1048576], P('scen', None, 'reach'), may hold values from -4 to 4
- resist: float32 [1048576], P('reach'), may hold values from 0.01 to 0.06
- flow_rate: float32 [8], P('scen'), may hold values from 3 to 5
- head_plan: float32 [8, 16], P('scen'), may hold values from -2 to 2
- valve_plan: float32 [8, 16], P('scen'), may hold values from 0.2 to 5
Outputs:
- basis_rows: float32 [2, 1048576, 128], P(None, ('reach', 'scen'))
- triangle: float32 [128, 128], replicated
All inputs are finite; a program needn't handle non-finite values.
Results may differ from a plain program's by a relative error of at most 0.0009.
The roundings to bfloat16 on the way count: a program that leaves them out, or rounds other values in their place, can miss the bound.
Values may be sent and summed in bfloat16 or wider, within the bound.
No kernel may reach another device: no remote copies, remote signals or barrier semaphores. Data moves between devices by JAX's collectives and lax.ppermute only.
A program may use at most 64 MiB of HBM per device.

v0:
```python
import jax
import jax.numpy as jnp
from jax import lax
from jax.sharding import PartitionSpec as P

STEPS = 16
BLOCK = 4


SHARES = (0.06, 0.04, 0.025, 0.015)
RETAINS = (0.2, 0.5, 0.8, 0.95)


def carried_in(value, axis, join, neutral):
    count, mine = (lax.axis_size(axis), lax.axis_index(axis))
    pieces = lax.all_gather(value, axis)
    total = jnp.full_like(value, 0) + jnp.asarray(neutral, value.dtype)

    def step(position, total):
        longer = join(total, pieces[position])
        return jnp.where(position < mine, longer, total)

    return lax.fori_loop(0, count - 1, step, total)


def shifted(value, axis, by):
    count = lax.axis_size(axis)
    pairs = [(i, i + by) for i in range(count) if 0 <= i + by < count]
    return lax.ppermute(value, axis, pairs)


def for_sending(value):
    return jax.tree.map(lambda a: a.astype(jnp.bfloat16) if a.dtype == jnp.float32 else a, value)


def carried(head_now, flow_now, states, resist):
    friction = resist * flow_now * jnp.abs(flow_now) + (
        states[0] + states[1] + states[2] + states[3]
    )
    return (head_now + flow_now - friction, head_now - flow_now + friction)


def update(current_flow, states, from_left, from_right, left_mask, right_mask, head_left, opening):
    new_head = 0.5 * (from_left + from_right)
    new_flow = 0.5 * (from_left - from_right)
    orifice = 1.0 / (1.0 + opening)
    new_head = jnp.where(left_mask, head_left, new_head)
    new_flow = jnp.where(left_mask, head_left - from_right, new_flow)
    new_head = jnp.where(right_mask, from_left * orifice, new_head)
    new_flow = jnp.where(right_mask, opening * from_left * orifice, new_flow)
    change = new_flow - current_flow
    new_states = tuple(
        (RETAINS[which] * states[which] + SHARES[which] * change for which in range(4))
    )
    return (new_head, new_flow, new_states)


def stepped_whole(perturb, resist, flow_rate, head_plan, valve_plan):
    cell_count = resist.shape[0]
    reaches = lax.axis_size("reach")
    reach_id = lax.axis_index("reach")
    total_cells = cell_count * reaches
    first_dev = reach_id == 0
    last_dev = reach_id == reaches - 1
    steady = flow_rate[0]
    running = jnp.cumsum(resist * (steady * jnp.abs(steady) / total_cells))
    upstream = carried_in(running[-1], "reach", jnp.add, jnp.float32(0.0))
    head_now = head_plan[0, 0] - (upstream + running) + perturb[0, 0]
    flow_now = steady * total_cells ** (-0.5) + perturb[0, 1]
    states = tuple((jnp.zeros((cell_count,), jnp.float32) for which in range(4)))
    block_count = STEPS // BLOCK
    roster = (
        jnp.stack([head_plan[0], valve_plan[0]]).reshape(2, block_count, BLOCK).transpose(1, 0, 2)
    )

    def run_block(previous, plan_block):
        head_cur, flow_cur, state_cur = previous
        frames = []
        position = jnp.arange(cell_count)
        left_mask = (position == 0) & first_dev
        right_mask = (position == cell_count - 1) & last_dev
        for moment in range(BLOCK):
            forward, backward = carried(head_cur, flow_cur, state_cur, resist)
            incoming_left = shifted(forward[cell_count - 1 :], "reach", 1)
            incoming_right = shifted(backward[:1], "reach", -1)
            from_left = jnp.concatenate([incoming_left, forward[:-1]])
            from_right = jnp.concatenate([backward[1:], incoming_right])
            head_cur, flow_cur, state_cur = update(
                flow_cur,
                state_cur,
                from_left,
                from_right,
                left_mask,
                right_mask,
                plan_block[0, moment],
                plan_block[1, moment],
            )
            frames.append(jnp.stack([head_cur, flow_cur]).astype(jnp.bfloat16))
        frames = jnp.stack(frames)
        return ((head_cur, flow_cur, state_cur), frames)

    finished, recorded = lax.scan(run_block, (head_now, flow_now, states), roster)
    columns = lax.all_to_all(
        for_sending(recorded.reshape(STEPS, 2, cell_count)),
        "scen",
        split_axis=2,
        concat_axis=0,
        tiled=True,
    )
    return columns


def local(perturb, resist, flow_rate, head_plan, valve_plan):
    total_cells = resist.shape[0] * lax.axis_size("reach")
    columns = stepped_whole(perturb, resist, flow_rate, head_plan, valve_plan)
    partial_value = jnp.einsum("cfr,dfr->cd", columns, columns, preferred_element_type=jnp.float32)
    summed = lax.psum(partial_value, ("scen", "reach"))
    moments = summed / (2 * total_cells)
    width_cols = moments.shape[0]
    factor_low = jnp.linalg.cholesky(moments)
    inverse = lax.linalg.triangular_solve(
        factor_low, jnp.eye(width_cols, dtype=jnp.float32), left_side=True, lower=True
    )
    basis_rows = jnp.einsum(
        "cfr,dc->frd",
        columns,
        inverse,
        precision=lax.Precision.HIGHEST,
        preferred_element_type=jnp.float32,
    )
    return (basis_rows, factor_low.T)


def solution(mesh):
    in_specs = (P("scen", None, "reach"), P("reach"), P("scen"), P("scen", None), P("scen", None))
    out_specs = (P(None, ("reach", "scen"), None), P())
    return jax.shard_map(local, mesh=mesh, in_specs=in_specs, out_specs=out_specs, check_vma=False)
```

profile of v0, /device:TPU:1, one launch (start us, length us, event | category | flops | bytes accessed | tf_op | source)
XLA Modules:
  0.0 961.7 jit_solution(16982826542077502108)
XLA Ops:
  12.3 123.3 %all-reduce = f32[64]{0:T(128)S(1)} all-reduce(f32[64]{0:T(128)S(1)} %slice_dynamic-update-slice_fusion), channel_id=1, replica_groups=mesh['scen'=8,'reach'=64] {'reach'}, use_global_device_ids=true, to_apply=%add | all-reduce | flops 64 | bytes 512
  135.6 73.8 %while.36 = (s32[]{:T(128)}, f32[]{:T(128)}, s32[]{:T(128)}, f32[64]{0:T(128)S(1)}, s32[]{:T(128)}) while((s32[]{:T(128)}, f32[]{:T(128)}, s32[]{:T(128)}, f32[64]{0:T(128)S(1)}, s32[]{:T(128)}) %tuple.100), condition=%wide.region_3.4_spmd, body=%wide.region_2.3_spmd.sunk | while | flops 5 | bytes 115 | solution.py:23
  211.1 309.2 %while.37 = (s32[]{:T(128)}, f32[16384]{0:T(1024)S(1)}, f32[16384]{0:T(1024)S(1)}, f32[16384]{0:T(1024)S(1)}, f32[16384]{0:T(1024)S(1)}, /*index=5*/f32[16384]{0...) while((s32[]{:T(128)}, f32[16384]{0:T(1024)S(1)}, ...), condition=%wide.region_5.6_spmd.clone, body=%wide.region_4.5_spmd.clone.sunk | while | flops 7847947 | bytes 8651816 | solution.py:102
  214.4 4.5 collective-permute-start.1
  224.5 2.7 convert_bitcast_fusion.22
  229.8 2.8 add_subtract_fusion.9
  237.1 4.6 collective-permute-start.3
  244.0 2.8 convert_bitcast_fusion.20
  246.8 3.5 add_subtract_fusion.10
  254.8 4.9 collective-permute-start.5
  262.1 2.8 convert_bitcast_fusion.18
  264.9 3.5 add_subtract_fusion.11
  273.0 4.8 collective-permute-start.7
  289.5 4.7 collective-permute-start.1
  305.0 2.8 add_subtract_fusion.9
  312.3 4.6 collective-permute-start.3
  319.2 2.8 convert_bitcast_fusion.20
  322.0 3.5 add_subtract_fusion.10
  330.1 4.9 collective-permute-start.5
  337.3 2.8 convert_bitcast_fusion.18
  340.1 3.5 add_subtract_fusion.11
  348.2 4.8 collective-permute-start.7
  364.7 5.8 collective-permute-start.1
  381.3 2.8 add_subtract_fusion.9
  388.6 5.5 collective-permute-start.3
  396.5 2.8 convert_bitcast_fusion.20
  399.2 3.5 add_subtract_fusion.10
  407.3 6.1 collective-permute-start.5
  415.8 2.8 convert_bitcast_fusion.18
  418.5 3.5 add_subtract_fusion.11
  426.7 5.9 collective-permute-start.7
  444.2 5.8 collective-permute-start.1
  460.8 2.8 add_subtract_fusion.9
  468.1 5.5 collective-permute-start.3
  475.9 2.8 convert_bitcast_fusion.20
  478.7 3.5 add_subtract_fusion.10
  486.8 6.1 collective-permute-start.5
  495.3 2.8 convert_bitcast_fusion.18
  498.0 3.5 add_subtract_fusion.11
  506.2 5.9 collective-permute-start.7
  520.4 12.8 %copy.38 = bf16[16,2,16384]{0,1,2:T(2,128)(2,1)} copy(bf16[16,2,16384]{2,1,0:T(2,128)(2,1)S(1)} %bitcast.200) | data formatting | bytes 2097152 | tf_op jit(solution)/shard_map/reshape | solution.py:104
  533.2 10.4 %reshape.1693 = bf16[8,2,32768]{2,1,0:T(2,128)(2,1)S(1)} reshape(bf16[16384,2,16]{2,1,0:T(2,128)(2,1)} %bitcast.190) | data formatting | bytes 2097152
  543.6 63.4 %all_to_all.18 = bf16[8,2,32768]{2,1,0:T(2,128)(2,1)S(1)} all-to-all(bf16[8,2,32768]{2,1,0:T(2,128)(2,1)S(1)} %reshape.1693), channel_id=1, replica_groups=mesh['scen'=8,'reach'=64] {'scen'}, dimensions={0} | all-to-all | bytes 2097152 | tf_op jit(solution)/shard_map/all_to_all | solution.py:103
  607.0 7.5 reshape.1694
  614.5 17.7 %copy.48 = bf16[16,2,8,2048]{3,0,2,1:T(8,128)(2,1)S(1)} copy(bf16[16,2,8,2048]{0,1,3,2:T(2,128)(2,1)} %bitcast.191) | data formatting | bytes 2097152 | tf_op jit(solution)/shard_map/all_to_all | solution.py:103
  633.3 293.4 %all-reduce.3.cloned.1.call-done = f32[128,128]{0,1:T(8,128)} async-done(((f32[128,128]{0,1:T(8,128)}), f32[128,128]{0,1:T(8,128)}) %all-reduce.3.cloned.1.call-update) | async-done | bytes 65552 | tf_op jit(solution)/shard_map/psum | solution.py:117
  928.5 11.7 %cholesky.17 = f32[128,128]{1,0:T(8,128)S(1)} custom-call(f32[128,128]{1,0:T(8,128)S(1)} %fusion.4), custom_call_target="Cholesky" | custom-call | tf_op jit(solution)/shard_map/jit(cholesky)/cholesky | solution.py:120
  942.3 9.8 %custom-call.6 = f32[1,128,128]{1,2,0:T(8,128)S(1)} custom-call(f32[1,128,128]{2,1,0:T(8,128)S(1)} %get-tuple-element.308), custom_call_target="InvertDiagBlocksLowerTriangular" | custom-call | tf_op jit(solution)/shard_map/triangular_solve | solution.py:121
  (259 shorter events, 199.8 us)
Async XLA Ops:
  7.2 919.5 %all-reduce.3.cloned.1.call-start = ((), (), s32[]{:S(2)}) async-start(), calls=%async_computation.1 | async-start | bytes 131072 | tf_op jit(solution)/shard_map/psum | solution.py:117
  212.5 9.8 %collective-permute-start = (f32[1]{0:T(128)}, f32[1]{0:T(128)}, u32[]{:S(2)}, u32[]{:S(2)}) collective-permute-start(f32[1]{0:T(128)} %slice.190), channel_id=1, source_target_pairs={{1,0},{2,1},{3,2},{4,3},{5,4},{6,5},{7,6},{8,7},{9,8},{10,9},{11,1... | collective-permute-start | bytes 20 | tf_op jit(solution)/shard_map/while/body/eval_jaxpr/ppermute | solution.py:29
  214.4 8.0 collective-permute-start.1
  235.8 5.9 collective-permute-start.2
  237.1 4.8 collective-permute-start.3
  253.6 6.2 collective-permute-start.4
  254.8 5.1 collective-permute-start.5
  271.8 6.1 collective-permute-start.6
  273.0 5.2 collective-permute-start.7
  287.6 10.0 %collective-permute-start = (f32[1]{0:T(128)}, f32[1]{0:T(128)}, u32[]{:S(2)}, u32[]{:S(2)}) collective-permute-start(f32[1]{0:T(128)} %slice.190), channel_id=1, source_target_pairs={{1,0},{2,1},{3,2},{4,3},{5,4},{6,5},{7,6},{8,7},{9,8},{10,9},{11,1... | collective-permute-start | bytes 20 | tf_op jit(solution)/shard_map/while/body/eval_jaxpr/ppermute | solution.py:29
  289.5 8.1 collective-permute-start.1
  311.0 5.9 collective-permute-start.2
  312.3 4.8 collective-permute-start.3
  328.8 6.2 collective-permute-start.4
  330.1 5.1 collective-permute-start.5
  347.0 6.1 collective-permute-start.6
  348.2 5.2 collective-permute-start.7
  362.8 11.0 %collective-permute-start = (f32[1]{0:T(128)}, f32[1]{0:T(128)}, u32[]{:S(2)}, u32[]{:S(2)}) collective-permute-start(f32[1]{0:T(128)} %slice.190), channel_id=1, source_target_pairs={{1,0},{2,1},{3,2},{4,3},{5,4},{6,5},{7,6},{8,7},{9,8},{10,9},{11,1... | collective-permute-start | bytes 20 | tf_op jit(solution)/shard_map/while/body/eval_jaxpr/ppermute | solution.py:29
  364.7 9.2 collective-permute-start.1
  387.3 6.8 collective-permute-start.2
  388.6 5.7 collective-permute-start.3
  406.0 7.4 collective-permute-start.4
  407.3 6.3 collective-permute-start.5
  425.4 7.2 collective-permute-start.6
  426.7 6.3 collective-permute-start.7
  442.3 11.0 %collective-permute-start = (f32[1]{0:T(128)}, f32[1]{0:T(128)}, u32[]{:S(2)}, u32[]{:S(2)}) collective-permute-start(f32[1]{0:T(128)} %slice.190), channel_id=1, source_target_pairs={{1,0},{2,1},{3,2},{4,3},{5,4},{6,5},{7,6},{8,7},{9,8},{10,9},{11,1... | collective-permute-start | bytes 20 | tf_op jit(solution)/shard_map/while/body/eval_jaxpr/ppermute | solution.py:29
  444.2 9.2 collective-permute-start.1
  466.8 6.8 collective-permute-start.2
  468.1 5.7 collective-permute-start.3
  485.5 7.4 collective-permute-start.4
  486.8 6.3 collective-permute-start.5
  504.9 7.2 collective-permute-start.6
  506.2 6.3 collective-permute-start.7
Sparse Core Ops, SparseCore 0:
  633.4 293.2 all-reduce.2
where the time goes:
time: 967 us; the launch traced here: 962 us
  waiting for transfers between devices  297 us (31%)
  other arithmetic  196 us (20%)
  blocking collectives  187 us (19%)
  local copies, waits for them, and re-layouts  110 us (11%)
  starting transfers between devices  105 us (11%)
  loops' own time  48.5 us (5%)
  between operations  14.8 us (2%)
    psum x1, waiting for transfers between devices, local(): summed = lax.psum(partial_value, ('scen', 'reach'))  293 us
    unnamed x1, blocking collectives  123 us
    ppermute x32, starting transfers between devices, shifted(): return lax.ppermute(value, axis, pairs)  105 us
    another operation x32, other arithmetic, run_block(): frames.append(jnp.stack([head_cur, flow_cur]).astype(jnp.bfloat16))  77.2 us
    all_to_all x1, blocking collectives, stepped_whole(): lax.all_to_all(for_sending(recorded.reshape(STEPS, 2, cell_count)), 'scen...  63.4 us
    sub x16, other arithmetic, carried(): return (head_now + flow_now - friction, head_now - flow_now + friction)  43 us
    another operation x1, loops' own time, carried_in(): return lax.fori_loop(0, count - 1, step, total)  37.3 us
    dynamic_slice x63, local copies, waits for them, and re-layouts, step(): longer = join(total, pieces[position])  36.5 us
  transfers between devices with their start and end apart: 33, of which 13 were waited for; matrix products, arithmetic and copies ran while one was open for 1% of the time, Pallas kernels for 0%

commit v1 on v0

v1 whole, which is shorter than its diff:
```python
import jax
import jax.numpy as jnp
from jax import lax
from jax.experimental import pallas as pl
from jax.experimental.pallas import tpu as pltpu
from jax.sharding import PartitionSpec as P

STEPS = 16
SHARES = (0.06, 0.04, 0.025, 0.015)
RETAINS = (0.2, 0.5, 0.8, 0.95)
LANES = 128
HALO = 16
SCENS = 8
REACHES = 64
COLS = SCENS * STEPS
CELLS = 1048576
PART = CELLS // REACHES
SHARE = PART // SCENS
BLOCKS = SHARE // LANES
RIGHT_ROW = 2 * BLOCKS
LEFT_ROW = RIGHT_ROW + 2
HEAD_ROW = LEFT_ROW + 2
VALVE_ROW = HEAD_ROW + 1
FLOW_ROW = VALVE_ROW + 1
WINDOW = 40
WIDE = BLOCKS + 2
PANEL = 32
CHUNK = 512
EXACT = lax.Precision.HIGHEST


def params():
    return pltpu.CompilerParams(vmem_limit_bytes=40 * 1024 * 1024)


def edges_kernel(state_ref, resist_ref, out_ref):
    lane = lax.broadcasted_iota(jnp.int32, (1, LANES), 1)
    last = 2 * PART // LANES - 2

    def ends(first, final):
        return jnp.where(lane < HALO, first, jnp.where(lane >= LANES - HALO, final, 0.0))

    resist = resist_ref[...]
    total = jnp.sum(jnp.sum(resist, axis=0, keepdims=True), axis=1, keepdims=True)
    row = jnp.concatenate(
        [
            ends(state_ref[0:1, :], state_ref[last : last + 1, :]),
            ends(state_ref[1:2, :], state_ref[last + 1 : last + 2, :]),
            ends(resist[0:1, :], resist[LANES - 1 : LANES, :]),
            jnp.broadcast_to(total, (1, LANES)),
        ],
        axis=0,
    )
    out_ref[...] = jnp.broadcast_to(row[None], (REACHES, 4, LANES))


def window_kernel(state_ref, resist_ref, edge_ref, flow_ref, head_ref, valve_ref, out_ref, aux_ref):
    reach = lax.axis_index("reach")
    scen = lax.axis_index("scen")
    left = edge_ref[jnp.maximum(reach - 1, 0)]
    right = edge_ref[jnp.minimum(reach + 1, REACHES - 1)]
    rows = 2 * BLOCKS
    for which in range(SCENS):
        start = which * rows
        out_ref[which, 0:rows, :] = state_ref[start : start + rows, :]
        if which < SCENS - 1:
            out_ref[which, RIGHT_ROW : RIGHT_ROW + 2, :] = state_ref[start + rows : start + rows + 2, :]
        else:
            out_ref[which, RIGHT_ROW : RIGHT_ROW + 2, :] = right[0:2]
        if which > 0:
            out_ref[which, LEFT_ROW : LEFT_ROW + 2, :] = state_ref[start - 2 : start, :]
        else:
            out_ref[which, LEFT_ROW : LEFT_ROW + 2, :] = left[0:2]
        out_ref[which, HEAD_ROW:WINDOW, :] = jnp.zeros((WINDOW - HEAD_ROW, LANES), jnp.float32)
        out_ref[which, HEAD_ROW : HEAD_ROW + 1, 0:STEPS] = head_ref[...]
        out_ref[which, VALVE_ROW : VALVE_ROW + 1, 0:STEPS] = valve_ref[...]
        out_ref[which, FLOW_ROW : FLOW_ROW + 1, :] = jnp.full((1, LANES), flow_ref[0], jnp.float32)

    first = scen * BLOCKS
    inner_left = resist_ref[pl.ds(jnp.maximum(first - 1, 0), 1), :]
    inner_right = resist_ref[pl.ds(jnp.minimum(first + BLOCKS, LANES - 1), 1), :]
    row_left = jnp.where(scen == 0, left[2:3], inner_left)
    row_right = jnp.where(scen == SCENS - 1, right[2:3], inner_right)
    mine = resist_ref[pl.ds(pl.multiple_of(first, BLOCKS), BLOCKS), :]
    spread = jnp.concatenate([mine, row_right, row_left, jnp.zeros((6, LANES), jnp.float32)], axis=0)
    place = lax.broadcasted_iota(jnp.int32, (REACHES, 1), 0)
    upstream = jnp.sum(jnp.where(place < reach, edge_ref[:, 3, :], 0.0), axis=0, keepdims=True)
    row_id = lax.broadcasted_iota(jnp.int32, (LANES, 1), 0)
    before = jnp.sum(jnp.where(row_id < first, resist_ref[...], 0.0), axis=0, keepdims=True)
    base = upstream + jnp.sum(before, axis=1, keepdims=True)
    a = lax.broadcasted_iota(jnp.int32, (LANES, LANES), 0)
    b = lax.broadcasted_iota(jnp.int32, (LANES, LANES), 1)
    upto = jnp.where(a <= b, 1.0, 0.0).astype(jnp.float32)
    inside = jnp.dot(spread, upto, precision=EXACT, preferred_element_type=jnp.float32)
    totals = jnp.sum(spread, axis=1, keepdims=True)
    c = lax.broadcasted_iota(jnp.int32, (24, 24), 0)
    d = lax.broadcasted_iota(jnp.int32, (24, 24), 1)
    ahead = jnp.where((d < c) & (c <= BLOCKS) & (d < BLOCKS), 1.0, 0.0)
    ahead = ahead - jnp.where((c == BLOCKS + 1) & (d == BLOCKS + 1), 1.0, 0.0)
    shift = jnp.dot(
        ahead.astype(jnp.float32),
        jnp.broadcast_to(totals, (24, LANES)),
        precision=EXACT,
        preferred_element_type=jnp.float32,
    )
    aux_ref[0:24, :] = spread
    aux_ref[24:48, :] = base + (shift + inside)


def step_kernel(win_ref, aux_ref, cols_ref, gram_ref, wide_ref, plan_ref, kept_ref):
    scen = lax.axis_index("scen")
    reach = lax.axis_index("reach")
    lane = lax.broadcasted_iota(jnp.int32, (SCENS, LANES), 1)
    at_first = (lane == 0) & (scen == 0) & (reach == 0)
    at_last = (lane == LANES - 1) & (scen == SCENS - 1) & (reach == REACHES - 1)
    is_low = lane == 0
    is_high = lane == LANES - 1

    def taken(row):
        return win_ref[pl.ds(row, SCENS, stride=WINDOW), :]

    head_plan = taken(HEAD_ROW)
    valve_plan = taken(VALVE_ROW)
    orifice = 1.0 / (1.0 + valve_plan)
    opened = valve_plan * orifice
    for moment in range(STEPS):
        for which, plan in enumerate((head_plan, orifice, opened)):
            plan_ref[which, moment * SCENS : (moment + 1) * SCENS, :] = jnp.broadcast_to(
                plan[:, moment : moment + 1], (SCENS, LANES)
            )
    steady = taken(FLOW_ROW)
    scale = steady * jnp.abs(steady) * (1.0 / CELLS)
    mean_flow = steady * CELLS ** (-0.5)
    first_head = plan_ref[0, 0:SCENS, :]
    rows = [LEFT_ROW] + [2 * j for j in range(BLOCKS)] + [RIGHT_ROW]
    aux_rows = [BLOCKS + 1] + list(range(BLOCKS)) + [BLOCKS]
    none = jnp.zeros((SCENS, LANES), jnp.float32)
    for j in range(WIDE):
        running = aux_ref[24 + aux_rows[j] : 25 + aux_rows[j], :]
        wide_ref[0, j] = first_head - running * scale + taken(rows[j])
        wide_ref[1, j] = mean_flow + taken(rows[j] + 1)
        for state in range(4):
            wide_ref[2 + state, j] = none
        wide_ref[6, j] = jnp.broadcast_to(aux_ref[aux_rows[j] : aux_rows[j] + 1, :], (SCENS, LANES))

    def one_step(moment, carry):
        plan_rows = pl.ds(pl.multiple_of(moment * SCENS, SCENS), SCENS)
        head_left = plan_ref[0, plan_rows, :]
        small = plan_ref[1, plan_rows, :]
        large = plan_ref[2, plan_rows, :]

        def sent(j):
            head, flow = wide_ref[0, j], wide_ref[1, j]
            friction = wide_ref[6, j] * flow * jnp.abs(flow) + (
                (wide_ref[2, j] + wide_ref[3, j]) + (wide_ref[4, j] + wide_ref[5, j])
            )
            net = flow - friction
            return pltpu.roll(head + net, 1, 1), pltpu.roll(head - net, LANES - 1, 1)

        forward_before, (forward, backward) = None, sent(0)
        for j in range(WIDE):
            forward_after, backward_after = sent(j + 1) if j + 1 < WIDE else (forward, backward)
            if forward_before is None:
                forward_before = forward
            from_left = jnp.where(is_low, forward_before, forward)
            from_right = jnp.where(is_high, backward_after, backward)
            new_head = 0.5 * (from_left + from_right)
            new_flow = 0.5 * (from_left - from_right)
            if j == 1:
                new_head = jnp.where(at_first, head_left, new_head)
                new_flow = jnp.where(at_first, head_left - from_right, new_flow)
            if j == BLOCKS:
                new_head = jnp.where(at_last, from_left * small, new_head)
                new_flow = jnp.where(at_last, from_left * large, new_flow)
            change = new_flow - wide_ref[1, j]
            wide_ref[0, j] = new_head
            wide_ref[1, j] = new_flow
            for state in range(4):
                wide_ref[2 + state, j] = RETAINS[state] * wide_ref[2 + state, j] + SHARES[state] * change
            if 1 <= j <= BLOCKS:
                kept_ref[0, j - 1, plan_rows, :] = new_head
                kept_ref[1, j - 1, plan_rows, :] = new_flow
            forward_before, forward, backward = forward, forward_after, backward_after
        return carry

    lax.fori_loop(0, STEPS, one_step, 0)

    for field in range(2):
        for j in range(BLOCKS):
            for which in range(SCENS):
                piece = kept_ref[field, j, pl.ds(which, STEPS, stride=SCENS), :]
                cols_ref[field, which * STEPS : (which + 1) * STEPS, j * LANES : (j + 1) * LANES] = piece.astype(
                    jnp.bfloat16
                )
    total = None
    for field in range(2):
        columns = cols_ref[field]
        part = lax.dot_general(columns, columns, (((1,), (1,)), ((), ())), preferred_element_type=jnp.float32)
        total = part if total is None else total + part
    gram_ref[...] = total.reshape(SCENS, STEPS, COLS)


def fold_kernel(in_ref, out_ref):
    count, copies = in_ref.shape[0], out_ref.shape[0]
    total = in_ref[0]
    for which in range(1, count):
        total = total + in_ref[which]
    for which in range(copies):
        out_ref[which] = total


def basis_kernel(gram_ref, cols_ref, rows_ref, tri_ref, work_ref, out_ref, sems):
    scale = 1.0 / (2 * CELLS)
    row_id = lax.broadcasted_iota(jnp.int32, (COLS, COLS), 0)
    col_id = lax.broadcasted_iota(jnp.int32, (COLS, COLS), 1)
    work_ref[:, 0:COLS] = gram_ref[...].reshape(COLS, COLS) * scale
    work_ref[:, COLS:] = jnp.where(row_id == col_id, 1.0, 0.0).astype(jnp.float32)
    sub = lax.broadcasted_iota(jnp.int32, (8, 1), 0)
    groups = PANEL // 8
    for panel in range(COLS // PANEL):
        low = panel * PANEL
        left = [work_ref[low + 8 * g : low + 8 * g + 8, 0:COLS] for g in range(groups)]
        right = [work_ref[low + 8 * g : low + 8 * g + 8, COLS:] for g in range(groups)]
        for k in range(PANEL):
            own, inner = divmod(k, 8)
            column = low + k
            row_left = left[own][inner : inner + 1, :]
            row_right = right[own][inner : inner + 1, :]
            inverse = 1.0 / row_left[:, column : column + 1]
            row_left = row_left * inverse
            row_right = row_right * inverse
            for g in range(own, groups):
                factor = left[g][:, column : column + 1]
                if g == own:
                    factor = jnp.where(sub > inner, factor, 0.0)
                left[g] = left[g] - factor * row_left
                right[g] = right[g] - factor * row_right
        for g in range(groups):
            work_ref[low + 8 * g : low + 8 * g + 8, 0:COLS] = left[g]
            work_ref[low + 8 * g : low + 8 * g + 8, COLS:] = right[g]
        if low + PANEL < COLS:
            rows = work_ref[low : low + PANEL, :]
            here = rows[:, 0:COLS]
            own_rows = lax.broadcasted_iota(jnp.int32, (PANEL, COLS), 0) + low
            own_cols = lax.broadcasted_iota(jnp.int32, (PANEL, COLS), 1)
            pivot = jnp.sum(jnp.where(own_rows == own_cols, here, 0.0), axis=1, keepdims=True)
            update = lax.dot_general(
                here / pivot,
                rows,
                (((0,), (0,)), ((), ())),
                precision=EXACT,
                preferred_element_type=jnp.float32,
            )
            work_ref[low + PANEL :, :] = work_ref[low + PANEL :, :] - update[low + PANEL :, :]
    reduced = work_ref[:, 0:COLS]
    pivot = jnp.sum(jnp.where(row_id == col_id, reduced, 0.0), axis=1, keepdims=True)
    root = 1.0 / jnp.sqrt(pivot)
    tri_ref[...] = jnp.where(row_id <= col_id, reduced * root, 0.0)
    inverse = (work_ref[:, COLS:] * root).T
    high = inverse.astype(jnp.bfloat16)
    rest = inverse - high.astype(jnp.float32)
    middle = rest.astype(jnp.bfloat16)
    low_part = (rest - middle.astype(jnp.float32)).astype(jnp.bfloat16)
    copies = []
    for field in range(2):
        for part in range(SHARE // CHUNK):
            piece = cols_ref[field, :, part * CHUNK : (part + 1) * CHUNK].T
            total = jnp.dot(piece, low_part, preferred_element_type=jnp.float32)
            total = total + jnp.dot(piece, middle, preferred_element_type=jnp.float32)
            total = total + jnp.dot(piece, high, preferred_element_type=jnp.float32)
            slot = len(copies)
            out_ref[slot] = total
            copy = pltpu.make_async_copy(
                out_ref.at[slot], rows_ref.at[field, pl.ds(part * CHUNK, CHUNK), :], sems.at[slot]
            )
            copy.start()
            copies.append(copy)
    for copy in copies:
        copy.wait()


def fold(value, copies):
    return pl.pallas_call(
        fold_kernel,
        out_shape=jax.ShapeDtypeStruct((copies,) + value.shape[1:], jnp.float32),
        compiler_params=params(),
    )(value)


def exchanged(value, axis):
    return lax.all_to_all(value, axis, split_axis=0, concat_axis=0, tiled=True)


def local(perturb, resist, flow_rate, head_plan, valve_plan):
    f32 = jnp.float32
    vmem = pl.BlockSpec(memory_space=pltpu.VMEM)
    smem = pl.BlockSpec(memory_space=pltpu.SMEM)
    blocks = PART // LANES
    state = perturb.reshape(2, blocks, LANES).transpose(1, 0, 2).reshape(2 * blocks, LANES)
    resist = resist.reshape(LANES, LANES)
    edges = pl.pallas_call(
        edges_kernel,
        out_shape=jax.ShapeDtypeStruct((REACHES, 4, LANES), f32),
        compiler_params=params(),
    )(state, resist)
    edges = exchanged(edges, "reach")
    windows, aux = pl.pallas_call(
        window_kernel,
        in_specs=[vmem, vmem, vmem, smem, vmem, vmem],
        out_shape=(
            jax.ShapeDtypeStruct((SCENS, WINDOW, LANES), f32),
            jax.ShapeDtypeStruct((48, LANES), f32),
        ),
        compiler_params=params(),
    )(state, resist, edges, flow_rate, head_plan, valve_plan)
    windows = exchanged(windows, "scen").reshape(SCENS * WINDOW, LANES)
    columns, gram = pl.pallas_call(
        step_kernel,
        out_shape=(
            jax.ShapeDtypeStruct((2, COLS, SHARE), jnp.bfloat16),
            jax.ShapeDtypeStruct((SCENS, STEPS, COLS), f32),
        ),
        scratch_shapes=[
            pltpu.VMEM((7, WIDE, SCENS, LANES), f32),
            pltpu.VMEM((3, STEPS * SCENS, LANES), f32),
            pltpu.VMEM((2, BLOCKS, COLS, LANES), f32),
        ],
        compiler_params=params(),
    )(windows, aux)
    gram = fold(exchanged(gram, "scen"), REACHES)
    gram = fold(exchanged(gram, "reach"), SCENS)
    gram = exchanged(gram, "scen")
    chunks = 2 * SHARE // CHUNK
    return pl.pallas_call(
        basis_kernel,
        in_specs=[vmem, vmem],
        out_specs=(pl.BlockSpec(memory_space=pl.ANY), vmem),
        out_shape=(
            jax.ShapeDtypeStruct((2, SHARE, COLS), f32),
            jax.ShapeDtypeStruct((COLS, COLS), f32),
        ),
        scratch_shapes=[
            pltpu.VMEM((COLS, 2 * COLS), f32),
            pltpu.VMEM((chunks, CHUNK, COLS), f32),
            pltpu.SemaphoreType.DMA((chunks,)),
        ],
        compiler_params=params(),
    )(gram, columns)


def solution(mesh):
    in_specs = (P("scen", None, "reach"), P("reach"), P("scen"), P("scen", None), P("scen", None))
    out_specs = (P(None, ("reach", "scen"), None), P())
    return jax.shard_map(local, mesh=mesh, in_specs=in_specs, out_specs=out_specs, check_vma=False)
```

time: 967 us -> 104 us (0.11)
  waiting for transfers between devices: 297 us -> 10.9 us
  other arithmetic: 196 us -> 0 us
  blocking collectives: 187 us -> 50.9 us
  local copies, waits for them, and re-layouts: 110 us -> 4.79 us
  starting transfers between devices: 105 us -> 17.1 us
  loops' own time: 48.5 us -> 0 us
  Pallas kernels: 0 us -> 18.6 us
  between operations: 14.8 us -> 1.32 us
    psum x1 -> x0, waiting for transfers between devices: 293 us -> none  [local(): summed = lax.psum(partial_value, ('scen', 'reach'))]
    unnamed x1 -> x0, blocking collectives: 123 us -> none
    ppermute x32 -> x0, starting transfers between devices: 105 us -> none  [shifted(): return lax.ppermute(value, axis, pairs)]
    another operation x41 -> x0, other arithmetic: 101 us -> none  [the longest x32 77.2 us: run_block(): frames.append(jnp.stack([head_cur, flow_cur]).astype(jnp.bfloat16))]
    sub x20 -> x0, other arithmetic: 53.4 us -> none  [the longest x16 43 us: carried(): return (head_now + flow_now - friction, head_now - flow_now + friction)]
    another operation x2 -> x0, loops' own time: 48.5 us -> none  [the longest x1 37.3 us: carried_in(): return lax.fori_loop(0, count - 1, step, total)]
    dynamic_slice x67 -> x0, local copies, waits for them, and re-layouts: 36.5 us -> none  [the longest x63 36.5 us: step(): longer = join(total, pieces[position])]
    add x26 -> x0, other arithmetic: 36.5 us -> none  [the longest x16 24.4 us: carried(): return (head_now + flow_now - friction, head_now - flow_now + friction)]
  transfers between devices with their start and end apart: 33 -> 1, of which waited for: 13 -> 1; matrix products, arithmetic and copies ran while one was open for 1% -> 0% of each run, Pallas kernels for 0% -> 0%
where the time goes in v1:
time: 104 us
  blocking collectives  50.9 us (49%)
  Pallas kernels  18.6 us (18%)
  starting transfers between devices  17.1 us (16%)
  waiting for transfers between devices  10.9 us (10%)
  local copies, waits for them, and re-layouts  4.79 us (5%)
  between operations  1.32 us (1%)
    all_to_all x4, blocking collectives, exchanged(): return lax.all_to_all(value, axis, split_axis=0, concat_axis=0, tiled=True)  50.9 us
    all_to_all x1, starting transfers between devices, exchanged(): return lax.all_to_all(value, axis, split_axis=0, concat_axis=0, tiled=True)  17.1 us
    pallas_call x1, Pallas kernels, local(): pl.pallas_call(basis_kernel, in_specs=[vmem, vmem], out_specs=(pl.BlockSp...  14.4 us
    all_to_all x1, waiting for transfers between devices, exchanged(): return lax.all_to_all(value, axis, split_axis=0, concat_axis=0, tiled=True)  10.9 us
    unnamed x12, local copies, waits for them, and re-layouts  4.79 us
    pallas_call x1, Pallas kernels, local(): pl.pallas_call(step_kernel, out_shape=(jax.ShapeDtypeStruct((2, COLS, SHA...  3.01 us
  transfers between devices with their start and end apart: 1, of which 1 were waited for; matrix products, arithmetic and copies ran while one was open for 0% of the time, Pallas kernels for 0%

profile of v1, /device:TPU:1, one launch (start us, length us, event | category | flops | bytes accessed | tf_op | source)
XLA Modules:
  0.0 103.6 jit_solution(16755082269373308456)
XLA Ops:
  0.6 0.0 copy-start
  0.6 0.9 copy-done
  1.5 0.0 copy-start.2
  1.5 0.8 copy-done.2
  2.4 0.8 shard_map.68
  3.1 17.1 %all-to-all-start = ((f32[64,4,128]{2,1,0:T(4,128)}), f32[64,4,128]{2,1,0:T(4,128)S(1)}, u32[]{:S(2)}, u32[]{:S(2)}) async-start(f32[64,4,128]{2,1,0:T(4,128)} %shard_map.68), calls=%async_computation | async-start | bytes 262144 | tf_op jit(solution)/shard_map/all_to_all | solution.py:291
  20.9 10.9 %all-to-all-done.edge_ref = f32[64,4,128]{2,1,0:T(4,128)S(1)} async-done(((f32[64,4,128]{2,1,0:T(4,128)}), f32[64,4,128]{2,1,0:T(4,128)S(1)}, u32[]{:S(2)}, u32[]{:S(2)}) %all-to-all-start) | async-done | bytes 131104 | tf_op jit(solution)/shard_map/all_to_all | solution.py:291
  31.8 0.0 copy-start.1
  31.8 0.9 copy-done.1
  32.7 0.0 copy-start.3
  32.7 0.8 copy-done.3
  33.5 0.0 copy-start.4
  33.5 0.7 copy-done.4
  34.2 0.0 copy-start.5
  34.2 0.7 copy-done.5
  34.8 0.2 shard_map.69
  35.1 11.8 %all_to_all.25 = f32[8,40,128]{2,1,0:T(8,128)S(1)} all-to-all(f32[8,40,128]{2,1,0:T(8,128)S(1)} %get-tuple-element.6), channel_id=1, replica_groups=mesh['scen'=8,'reach'=64] {'scen'}, dimensions={0} | all-to-all | bytes 327680 | tf_op jit(solution)/shard_map/all_to_all | solution.py:291
  46.9 3.0 %shard_map.70 = (bf16[2,128,2048]{2,1,0:T(8,128)(2,1)S(1)}, f32[8,16,128]{2,1,0:T(8,128)S(1)}) custom-call(f32[320,128]{1,0:T(8,128)S(1)} %bitcast.7, f32[48,128]{1,0:T(8,128)S(1)} %get-tuple-element.7.aux_ref), custom_call_target="tpu_custom_call" | custom-call | tf_op jit(solution)/shard_map/pallas_call | solution.py:317
  50.0 8.1 %all_to_all.26.in_ref = f32[8,16,128]{2,1,0:T(8,128)S(1)} all-to-all(f32[8,16,128]{2,1,0:T(8,128)S(1)} %get-tuple-element.8), channel_id=1, replica_groups=mesh['scen'=8,'reach'=64] {'scen'}, dimensions={0} | all-to-all | bytes 131072 | tf_op jit(solution)/shard_map/all_to_all | solution.py:291
  58.1 20.3 %all_to_all.27.in_ref = f32[64,16,128]{2,1,0:T(8,128)S(1)} all-to-all(f32[64,16,128]{2,1,0:T(8,128)S(1)} %shard_map.71), channel_id=1, replica_groups=mesh['scen'=8,'reach'=64] {'reach'}, dimensions={0} | all-to-all | bytes 1048576 | tf_op jit(solution)/shard_map/all_to_all | solution.py:291
  78.5 0.1 shard_map.72
  78.5 10.6 %all_to_all.28.gram_ref = f32[8,16,128]{2,1,0:T(8,128)S(1)} all-to-all(f32[8,16,128]{2,1,0:T(8,128)S(1)} %shard_map.72), channel_id=1, replica_groups=mesh['scen'=8,'reach'=64] {'scen'}, dimensions={0} | all-to-all | bytes 131072 | tf_op jit(solution)/shard_map/all_to_all | solution.py:291
  89.2 14.4 %shard_map.73 = (f32[2,2048,128]{2,1,0:T(8,128)}, f32[128,128]{1,0:T(8,128)}) custom-call(f32[8,16,128]{2,1,0:T(8,128)S(1)} %all_to_all.28.gram_ref, bf16[2,128,2048]{2,1,0:T(8,128)(2,1)S(1)} %get-tuple-element.9.cols_ref), custom_call_target="tpu_custom_call" | custom-call | tf_op jit(solution)/shard_map/pallas_call | solution.py:334
  (1 shorter events, 0.0 us)
Async XLA Ops:
  0.6 0.9 copy-start
  1.5 0.8 copy-start.2
  3.1 28.6 %all-to-all-start = ((f32[64,4,128]{2,1,0:T(4,128)}), f32[64,4,128]{2,1,0:T(4,128)S(1)}, u32[]{:S(2)}, u32[]{:S(2)}) async-start(f32[64,4,128]{2,1,0:T(4,128)} %shard_map.68), calls=%async_computation | async-start | bytes 262144 | tf_op jit(solution)/shard_map/all_to_all | solution.py:291
  31.8 0.9 copy-start.1
  32.7 0.8 copy-start.3
  33.5 0.7 copy-start.4
  34.2 0.7 copy-start.5

commit v2 on v1

--- a/solution.py
+++ b/solution.py
@@ -24,70 +24,61 @@
 FLOW_ROW = VALVE_ROW + 1
 WINDOW = 40
 WIDE = BLOCKS + 2
-PANEL = 32
-CHUNK = 512
+PANEL = 64
+CHUNK = 256
 EXACT = lax.Precision.HIGHEST
 
 
-def params():
-    return pltpu.CompilerParams(vmem_limit_bytes=40 * 1024 * 1024)
-
-
-def edges_kernel(state_ref, resist_ref, out_ref):
+def params(mib=40):
+    return pltpu.CompilerParams(vmem_limit_bytes=mib * 1024 * 1024)
+
+
+def prepare_kernel(state_hbm, resist_hbm, flow_hbm, head_hbm, valve_hbm, edge_ref, out_ref, state, resist, flow, head, valve, sems):
+    loads = []
+    for which, (source, target) in enumerate(
+        ((resist_hbm, resist), (state_hbm, state), (flow_hbm, flow), (head_hbm, head), (valve_hbm, valve))
+    ):
+        copy = pltpu.make_async_copy(source, target, sems.at[which])
+        copy.start()
+        loads.append(copy)
+    loads[0].wait()
     lane = lax.broadcasted_iota(jnp.int32, (1, LANES), 1)
-    last = 2 * PART // LANES - 2
-
-    def ends(first, final):
-        return jnp.where(lane < HALO, first, jnp.where(lane >= LANES - HALO, final, 0.0))
-
-    resist = resist_ref[...]
-    total = jnp.sum(jnp.sum(resist, axis=0, keepdims=True), axis=1, keepdims=True)
-    row = jnp.concatenate(
-        [
-            ends(state_ref[0:1, :], state_ref[last : last + 1, :]),
-            ends(state_ref[1:2, :], state_ref[last + 1 : last + 2, :]),
-            ends(resist[0:1, :], resist[LANES - 1 : LANES, :]),
-            jnp.broadcast_to(total, (1, LANES)),
-        ],
-        axis=0,
+    total = jnp.sum(jnp.sum(resist[...], axis=0, keepdims=True), axis=1, keepdims=True)
+    ends = jnp.where(
+        lane < HALO, resist[0:1, :], jnp.where(lane >= LANES - HALO, resist[LANES - 1 : LANES, :], 0.0)
     )
-    out_ref[...] = jnp.broadcast_to(row[None], (REACHES, 4, LANES))
-
-
-def window_kernel(state_ref, resist_ref, edge_ref, flow_ref, head_ref, valve_ref, out_ref, aux_ref):
-    reach = lax.axis_index("reach")
-    scen = lax.axis_index("scen")
-    left = edge_ref[jnp.maximum(reach - 1, 0)]
-    right = edge_ref[jnp.minimum(reach + 1, REACHES - 1)]
+    upto = ends
+    for step in (1, 2, 4, 8):
+        upto = upto + jnp.where(lane >= step, pltpu.roll(upto, step, 1), 0.0)
+    upto = jnp.where(lane < HALO, upto, upto - upto[:, LANES - 1 : LANES])
+    row = jnp.concatenate([ends, upto, jnp.broadcast_to(total, (1, LANES)), ends], axis=0)
+    edge_ref[...] = jnp.broadcast_to(row[None], (REACHES, 4, LANES))
+    for copy in loads[1:]:
+        copy.wait()
     rows = 2 * BLOCKS
+    none = jnp.zeros((2, LANES), jnp.float32)
     for which in range(SCENS):
         start = which * rows
-        out_ref[which, 0:rows, :] = state_ref[start : start + rows, :]
-        if which < SCENS - 1:
-            out_ref[which, RIGHT_ROW : RIGHT_ROW + 2, :] = state_ref[start + rows : start + rows + 2, :]
-        else:
-            out_ref[which, RIGHT_ROW : RIGHT_ROW + 2, :] = right[0:2]
-        if which > 0:
-            out_ref[which, LEFT_ROW : LEFT_ROW + 2, :] = state_ref[start - 2 : start, :]
-        else:
-            out_ref[which, LEFT_ROW : LEFT_ROW + 2, :] = left[0:2]
+        out_ref[which, 0:rows, :] = state[start : start + rows, :]
+        after = state[start + rows : start + rows + 2, :] if which < SCENS - 1 else none
+        out_ref[which, RIGHT_ROW : RIGHT_ROW + 2, :] = after
+        out_ref[which, LEFT_ROW : LEFT_ROW + 2, :] = state[start - 2 : start, :] if which > 0 else none
         out_ref[which, HEAD_ROW:WINDOW, :] = jnp.zeros((WINDOW - HEAD_ROW, LANES), jnp.float32)
-        out_ref[which, HEAD_ROW : HEAD_ROW + 1, 0:STEPS] = head_ref[...]
-        out_ref[which, VALVE_ROW : VALVE_ROW + 1, 0:STEPS] = valve_ref[...]
-        out_ref[which, FLOW_ROW : FLOW_ROW + 1, :] = jnp.full((1, LANES), flow_ref[0], jnp.float32)
-
+        out_ref[which, HEAD_ROW : HEAD_ROW + 1, 0:STEPS] = head[...]
+        out_ref[which, VALVE_ROW : VALVE_ROW + 1, 0:STEPS] = valve[...]
+        out_ref[which, FLOW_ROW : FLOW_ROW + 1, :] = jnp.full((1, LANES), flow[0], jnp.float32)
+
+
+def spread_kernel(resist_ref, aux_ref):
+    scen = lax.axis_index("scen")
     first = scen * BLOCKS
-    inner_left = resist_ref[pl.ds(jnp.maximum(first - 1, 0), 1), :]
-    inner_right = resist_ref[pl.ds(jnp.minimum(first + BLOCKS, LANES - 1), 1), :]
-    row_left = jnp.where(scen == 0, left[2:3], inner_left)
-    row_right = jnp.where(scen == SCENS - 1, right[2:3], inner_right)
+    row_left = resist_ref[pl.ds(jnp.maximum(first - 1, 0), 1), :]
+    row_right = resist_ref[pl.ds(jnp.minimum(first + BLOCKS, LANES - 1), 1), :]
     mine = resist_ref[pl.ds(pl.multiple_of(first, BLOCKS), BLOCKS), :]
     spread = jnp.concatenate([mine, row_right, row_left, jnp.zeros((6, LANES), jnp.float32)], axis=0)
-    place = lax.broadcasted_iota(jnp.int32, (REACHES, 1), 0)
-    upstream = jnp.sum(jnp.where(place < reach, edge_ref[:, 3, :], 0.0), axis=0, keepdims=True)
     row_id = lax.broadcasted_iota(jnp.int32, (LANES, 1), 0)
     before = jnp.sum(jnp.where(row_id < first, resist_ref[...], 0.0), axis=0, keepdims=True)
-    base = upstream + jnp.sum(before, axis=1, keepdims=True)
+    base = jnp.sum(before, axis=1, keepdims=True)
     a = lax.broadcasted_iota(jnp.int32, (LANES, LANES), 0)
     b = lax.broadcasted_iota(jnp.int32, (LANES, LANES), 1)
     upto = jnp.where(a <= b, 1.0, 0.0).astype(jnp.float32)
@@ -107,7 +98,15 @@
     aux_ref[24:48, :] = base + (shift + inside)
 
 
-def step_kernel(win_ref, aux_ref, cols_ref, gram_ref, wide_ref, plan_ref, kept_ref):
+def outer_kernel(win_ref, out_ref):
+    low = lax.axis_index("scen") == 0
+    for field in range(2):
+        first = win_ref[pl.ds(field, SCENS, stride=WINDOW), :]
+        final = win_ref[pl.ds(RIGHT_ROW - 2 + field, SCENS, stride=WINDOW), :]
+        out_ref[field * SCENS : (field + 1) * SCENS, :] = jnp.where(low, first, final)
+
+
+def step_kernel(win_ref, outer_ref, edge_ref, aux_ref, cols_ref, gram_ref, wide_ref, plan_ref, kept_ref):
     scen = lax.axis_index("scen")
     reach = lax.axis_index("reach")
     lane = lax.broadcasted_iota(jnp.int32, (SCENS, LANES), 1)
@@ -132,16 +131,32 @@
     scale = steady * jnp.abs(steady) * (1.0 / CELLS)
     mean_flow = steady * CELLS ** (-0.5)
     first_head = plan_ref[0, 0:SCENS, :]
-    rows = [LEFT_ROW] + [2 * j for j in range(BLOCKS)] + [RIGHT_ROW]
-    aux_rows = [BLOCKS + 1] + list(range(BLOCKS)) + [BLOCKS]
+    place = lax.broadcasted_iota(jnp.int32, (REACHES, 1), 0)
+    totals = edge_ref[:, 2, :]
+    upstream = jnp.sum(jnp.where(place < reach, totals, 0.0), axis=0, keepdims=True)
+    through = jnp.sum(jnp.where(place <= reach, totals, 0.0), axis=0, keepdims=True)
+    previous = edge_ref[jnp.maximum(reach - 1, 0)]
+    following = edge_ref[jnp.minimum(reach + 1, REACHES - 1)]
     none = jnp.zeros((SCENS, LANES), jnp.float32)
     for j in range(WIDE):
-        running = aux_ref[24 + aux_rows[j] : 25 + aux_rows[j], :]
-        wide_ref[0, j] = first_head - running * scale + taken(rows[j])
-        wide_ref[1, j] = mean_flow + taken(rows[j] + 1)
+        row = [LEFT_ROW, RIGHT_ROW][j > BLOCKS] if j in (0, WIDE - 1) else 2 * (j - 1)
+        at = [BLOCKS + 1, BLOCKS][j > BLOCKS] if j in (0, WIDE - 1) else j - 1
+        resist = aux_ref[at : at + 1, :]
+        running = upstream + aux_ref[24 + at : 25 + at, :]
+        head, flow = taken(row), taken(row + 1)
+        if j in (0, WIDE - 1):
+            beyond, edge, base = (
+                (scen == 0, previous, upstream) if j == 0 else (scen == SCENS - 1, following, through)
+            )
+            resist = jnp.where(beyond, edge[0:1], resist)
+            running = jnp.where(beyond, base + edge[1:2], running)
+            head = jnp.where(beyond, outer_ref[0:SCENS, :], head)
+            flow = jnp.where(beyond, outer_ref[SCENS:, :], flow)
+        wide_ref[0, j] = first_head - running * scale + head
+        wide_ref[1, j] = mean_flow + flow
         for state in range(4):
             wide_ref[2 + state, j] = none
-        wide_ref[6, j] = jnp.broadcast_to(aux_ref[aux_rows[j] : aux_rows[j] + 1, :], (SCENS, LANES))
+        wide_ref[6, j] = jnp.broadcast_to(resist, (SCENS, LANES))
 
     def one_step(moment, carry):
         plan_rows = pl.ds(pl.multiple_of(moment * SCENS, SCENS), SCENS)
@@ -211,65 +226,64 @@
 
 def basis_kernel(gram_ref, cols_ref, rows_ref, tri_ref, work_ref, out_ref, sems):
     scale = 1.0 / (2 * CELLS)
-    row_id = lax.broadcasted_iota(jnp.int32, (COLS, COLS), 0)
-    col_id = lax.broadcasted_iota(jnp.int32, (COLS, COLS), 1)
+    sub = lax.broadcasted_iota(jnp.int32, (8, COLS), 0)
+    lane = lax.broadcasted_iota(jnp.int32, (8, COLS), 1)
+    groups = PANEL // 8
     work_ref[:, 0:COLS] = gram_ref[...].reshape(COLS, COLS) * scale
-    work_ref[:, COLS:] = jnp.where(row_id == col_id, 1.0, 0.0).astype(jnp.float32)
-    sub = lax.broadcasted_iota(jnp.int32, (8, 1), 0)
-    groups = PANEL // 8
-    for panel in range(COLS // PANEL):
-        low = panel * PANEL
+    for g in range(COLS // 8):
+        work_ref[8 * g : 8 * g + 8, COLS:] = jnp.where(lane == sub + 8 * g, 1.0, 0.0).astype(jnp.float32)
+    inverse_rows = []
+    for low in range(0, COLS, PANEL):
         left = [work_ref[low + 8 * g : low + 8 * g + 8, 0:COLS] for g in range(groups)]
         right = [work_ref[low + 8 * g : low + 8 * g + 8, COLS:] for g in range(groups)]
-        for k in range(PANEL):
-            own, inner = divmod(k, 8)
-            column = low + k
-            row_left = left[own][inner : inner + 1, :]
-            row_right = right[own][inner : inner + 1, :]
-            inverse = 1.0 / row_left[:, column : column + 1]
-            row_left = row_left * inverse
-            row_right = row_right * inverse
-            for g in range(own, groups):
-                factor = left[g][:, column : column + 1]
-                if g == own:
-                    factor = jnp.where(sub > inner, factor, 0.0)
-                left[g] = left[g] - factor * row_left
-                right[g] = right[g] - factor * row_right
-        for g in range(groups):
-            work_ref[low + 8 * g : low + 8 * g + 8, 0:COLS] = left[g]
-            work_ref[low + 8 * g : low + 8 * g + 8, COLS:] = right[g]
+        scaled = []
+        for own in range(groups):
+            start = low + 8 * own
+            wide = {
+                g: [jnp.broadcast_to(left[g][:, start + j : start + j + 1], (8, COLS)) for j in range(8)]
+                for g in range(own, groups)
+            }
+            inverses = jnp.zeros((8, COLS), jnp.float32)
+            for k in range(8):
+                inverse = 1.0 / wide[own][k][k : k + 1, :]
+                inverses = jnp.where(sub == k, inverse, inverses)
+                ahead = {j: wide[own][j][k : k + 1, :] * inverse for j in range(k + 1, 8)}
+                row_left = left[own][k : k + 1, :] * inverse
+                row_right = right[own][k : k + 1, :] * inverse
+                for g in range(own, groups):
+                    factor = wide[g][k]
+                    if g == own:
+                        factor = jnp.where(sub > k, factor, 0.0)
+                    for j in ahead:
+                        wide[g][j] = wide[g][j] - factor * ahead[j]
+                    left[g] = left[g] - factor * row_left
+                    right[g] = right[g] - factor * row_right
+            scaled.append(left[own] * inverses)
+            root = jnp.sqrt(inverses)
+            tri_ref[start : start + 8, :] = jnp.where(lane >= sub + start, left[own] * root, 0.0)
+            inverse_rows.append(right[own] * root)
         if low + PANEL < COLS:
-            rows = work_ref[low : low + PANEL, :]
-            here = rows[:, 0:COLS]
-            own_rows = lax.broadcasted_iota(jnp.int32, (PANEL, COLS), 0) + low
-            own_cols = lax.broadcasted_iota(jnp.int32, (PANEL, COLS), 1)
-            pivot = jnp.sum(jnp.where(own_rows == own_cols, here, 0.0), axis=1, keepdims=True)
             update = lax.dot_general(
-                here / pivot,
-                rows,
+                jnp.concatenate(scaled, axis=0),
+                jnp.concatenate([jnp.concatenate(left, axis=0), jnp.concatenate(right, axis=0)], axis=1),
                 (((0,), (0,)), ((), ())),
                 precision=EXACT,
                 preferred_element_type=jnp.float32,
             )
             work_ref[low + PANEL :, :] = work_ref[low + PANEL :, :] - update[low + PANEL :, :]
-    reduced = work_ref[:, 0:COLS]
-    pivot = jnp.sum(jnp.where(row_id == col_id, reduced, 0.0), axis=1, keepdims=True)
-    root = 1.0 / jnp.sqrt(pivot)
-    tri_ref[...] = jnp.where(row_id <= col_id, reduced * root, 0.0)
-    inverse = (work_ref[:, COLS:] * root).T
+    inverse = jnp.concatenate(inverse_rows, axis=0).T
     high = inverse.astype(jnp.bfloat16)
     rest = inverse - high.astype(jnp.float32)
     middle = rest.astype(jnp.bfloat16)
-    low_part = (rest - middle.astype(jnp.float32)).astype(jnp.bfloat16)
+    both = jnp.concatenate([high, middle], axis=0)
     copies = []
     for field in range(2):
         for part in range(SHARE // CHUNK):
             piece = cols_ref[field, :, part * CHUNK : (part + 1) * CHUNK].T
-            total = jnp.dot(piece, low_part, preferred_element_type=jnp.float32)
-            total = total + jnp.dot(piece, middle, preferred_element_type=jnp.float32)
-            total = total + jnp.dot(piece, high, preferred_element_type=jnp.float32)
             slot = len(copies)
-            out_ref[slot] = total
+            out_ref[slot] = jnp.dot(
+                jnp.concatenate([piece, piece], axis=1), both, preferred_element_type=jnp.float32
+            )
             copy = pltpu.make_async_copy(
                 out_ref.at[slot], rows_ref.at[field, pl.ds(part * CHUNK, CHUNK), :], sems.at[slot]
             )
@@ -294,26 +308,39 @@
 def local(perturb, resist, flow_rate, head_plan, valve_plan):
     f32 = jnp.float32
     vmem = pl.BlockSpec(memory_space=pltpu.VMEM)
-    smem = pl.BlockSpec(memory_space=pltpu.SMEM)
+    hbm = pl.BlockSpec(memory_space=pltpu.HBM)
     blocks = PART // LANES
     state = perturb.reshape(2, blocks, LANES).transpose(1, 0, 2).reshape(2 * blocks, LANES)
     resist = resist.reshape(LANES, LANES)
-    edges = pl.pallas_call(
-        edges_kernel,
-        out_shape=jax.ShapeDtypeStruct((REACHES, 4, LANES), f32),
-        compiler_params=params(),
-    )(state, resist)
+    edges, windows = pl.pallas_call(
+        prepare_kernel,
+        in_specs=[hbm] * 5,
+        out_specs=(vmem, vmem),
+        out_shape=(
+            jax.ShapeDtypeStruct((REACHES, 4, LANES), f32),
+            jax.ShapeDtypeStruct((SCENS, WINDOW, LANES), f32),
+        ),
+        scratch_shapes=[
+            pltpu.VMEM((2 * blocks, LANES), f32),
+            pltpu.VMEM((LANES, LANES), f32),
+            pltpu.SMEM((1,), f32),
+            pltpu.VMEM((1, STEPS), f32),
+            pltpu.VMEM((1, STEPS), f32),
+            pltpu.SemaphoreType.DMA((5,)),
+        ],
+        compiler_params=params(60),
+    )(state, resist, flow_rate, head_plan, valve_plan)
     edges = exchanged(edges, "reach")
-    windows, aux = pl.pallas_call(
-        window_kernel,
-        in_specs=[vmem, vmem, vmem, smem, vmem, vmem],
-        out_shape=(
-            jax.ShapeDtypeStruct((SCENS, WINDOW, LANES), f32),
-            jax.ShapeDtypeStruct((48, LANES), f32),
-        ),
-        compiler_params=params(),
-    )(state, resist, edges, flow_rate, head_plan, valve_plan)
+    aux = pl.pallas_call(
+        spread_kernel, out_shape=jax.ShapeDtypeStruct((48, LANES), f32), compiler_params=params()
+    )(resist)
     windows = exchanged(windows, "scen").reshape(SCENS * WINDOW, LANES)
+    outer = pl.pallas_call(
+        outer_kernel, out_shape=jax.ShapeDtypeStruct((2 * SCENS, LANES), f32), compiler_params=params()
+    )(windows)
+    top = (SCENS - 1) * REACHES
+    pairs = [(top + r, r + 1) for r in range(REACHES - 1)]
+    outer = lax.ppermute(outer, ("scen", "reach"), pairs + [(b, a) for a, b in pairs])
     columns, gram = pl.pallas_call(
         step_kernel,
         out_shape=(
@@ -326,7 +353,7 @@
             pltpu.VMEM((2, BLOCKS, COLS, LANES), f32),
         ],
         compiler_params=params(),
-    )(windows, aux)
+    )(windows, outer, edges, aux)
     gram = fold(exchanged(gram, "scen"), REACHES)
     gram = fold(exchanged(gram, "reach"), SCENS)
     gram = exchanged(gram, "scen")

time: 104 us -> 96.7 us (0.930)
  blocking collectives: 50.9 us -> 60.6 us
  Pallas kernels: 18.6 us -> 11.1 us
  starting transfers between devices: 17.1 us -> 12.6 us
  local copies, waits for them, and re-layouts: 4.79 us -> 0.83 us
  waiting for transfers between devices: 10.9 us -> 9.82 us
    all_to_all x4, blocking collectives: 50.9 us -> 60.6 us  [exchanged(): return lax.all_to_all(value, axis, split_axis=0, concat_axis=0, tiled=True)]
    pallas_call x1, Pallas kernels: 14.4 us -> 5.71 us  [local(): pl.pallas_call(basis_kernel, in_specs=[vmem, vmem], out_specs=(pl.BlockSp...]
    all_to_all x1, starting transfers between devices: 17.1 us -> 11.9 us  [exchanged(): return lax.all_to_all(value, axis, split_axis=0, concat_axis=0, tiled=True)]
    unnamed x12 -> x2, local copies, waits for them, and re-layouts: 4.79 us -> 0.83 us
    pallas_call x2 -> x3, Pallas kernels: 1.01 us -> 2.21 us  [the longest x1 1.98 us: local(): pl.pallas_call(prepare_kernel, in_specs=[hbm] * 5, out_specs=(vmem, vmem)...]
  transfers between devices with their start and end apart: 1 -> 2, of which waited for: 1 -> 1; matrix products, arithmetic and copies ran while one was open for 0% -> 0% of each run, Pallas kernels for 0% -> 0%
where the time goes in v2:
time: 96.7 us; the launch traced here: 96.3 us
  blocking collectives  60.6 us (63%)
  starting transfers between devices  12.6 us (13%)
  Pallas kernels  11.1 us (11%)
  waiting for transfers between devices  9.82 us (10%)
  between operations  1.35 us (1%)
    all_to_all x4, blocking collectives, exchanged(): return lax.all_to_all(value, axis, split_axis=0, concat_axis=0, tiled=True)  60.6 us
    all_to_all x1, starting transfers between devices, exchanged(): return lax.all_to_all(value, axis, split_axis=0, concat_axis=0, tiled=True)  11.9 us
    all_to_all x1, waiting for transfers between devices, exchanged(): return lax.all_to_all(value, axis, split_axis=0, concat_axis=0, tiled=True)  9.82 us
    pallas_call x1, Pallas kernels, local(): pl.pallas_call(basis_kernel, in_specs=[vmem, vmem], out_specs=(pl.BlockSp...  5.71 us
    pallas_call x1, Pallas kernels, local(): pl.pallas_call(step_kernel, out_shape=(jax.ShapeDtypeStruct((2, COLS, SHA...  3.03 us
    pallas_call x1, Pallas kernels, local(): pl.pallas_call(prepare_kernel, in_specs=[hbm] * 5, out_specs=(vmem, vmem)...  1.98 us
  transfers between devices with their start and end apart: 2, of which 1 were waited for; matrix products, arithmetic and copies ran while one was open for 0% of the time, Pallas kernels for 0%

profile of v2, /device:TPU:1, one launch (start us, length us, event | category | flops | bytes accessed | tf_op | source)
XLA Modules:
  0.0 96.3 jit_solution(15091276086580774129)
XLA Ops:
  1.3 2.0 %shard_map.68 = (f32[64,4,128]{2,1,0:T(4,128)}, f32[8,40,128]{2,1,0:T(8,128)}) custom-call(f32[256,128]{1,0:T(8,128)} %bitcast.11, f32[128,128]{1,0:T(8,128)} %bitcast.9, f32[1]{0:T(128)S(6)} %copy.8.flow_hbm, f32[1,16]{1,0:T(1,128)} %head_hbm.1, f32[1,16]{1,0:T(1,128)} %valve_hbm.1), custom_call_target="tpu_custom_call" | custom-call | tf_op jit(solution)/shard_map/pallas_call | solution.py:315
  3.3 15.7 %all_to_all.25 = f32[8,40,128]{2,1,0:T(8,128)S(1)} all-to-all(f32[8,40,128]{2,1,0:T(8,128)} %get-tuple-element.6), channel_id=1, replica_groups=mesh['scen'=8,'reach'=64] {'scen'}, dimensions={0} | all-to-all | bytes 327680 | tf_op jit(solution)/shard_map/all_to_all | solution.py:305
  19.0 11.9 %all-to-all-start.1 = ((f32[64,4,128]{2,1,0:T(4,128)}), f32[64,4,128]{2,1,0:T(4,128)S(1)}, u32[]{:S(2)}, u32[]{:S(2)}) async-start(f32[64,4,128]{2,1,0:T(4,128)} %get-tuple-element.7), calls=%async_computation.1 | async-start | bytes 262144 | tf_op jit(solution)/shard_map/all_to_all | solution.py:305
  31.0 0.7 collective-permute-start
  31.7 0.0 copy-start
  31.7 0.8 copy-done
  32.5 0.2 shard_map.70.aux_ref
  32.7 0.0 collective-permute-done.outer_ref
  32.7 9.8 %all-to-all-done.1.edge_ref = f32[64,4,128]{2,1,0:T(4,128)S(1)} async-done(((f32[64,4,128]{2,1,0:T(4,128)}), f32[64,4,128]{2,1,0:T(4,128)S(1)}, u32[]{:S(2)}, u32[]{:S(2)}) %all-to-all-start.1) | async-done | bytes 131104 | tf_op jit(solution)/shard_map/all_to_all | solution.py:305
  42.5 3.0 %shard_map.71 = (bf16[2,128,2048]{2,1,0:T(8,128)(2,1)S(1)}, f32[8,16,128]{2,1,0:T(8,128)S(1)}) custom-call(f32[320,128]{1,0:T(8,128)S(1)} %bitcast.8, f32[16,128]{1,0:T(8,128)S(1)} %collective-permute-done.outer_ref, f32[64,4,128]{2,1,0:T(4,128)S(1)} %all-to-all-done.1.edge_ref, f32[48,128]{1,0:T(8,128)S(1)} %shard_map.70.aux_ref), custom_call_target="tpu_custom_call" | custom-call | tf_op jit(solution)/shard_map/pallas_call | solution.py:344
  45.6 9.4 %all_to_all.26.in_ref = f32[8,16,128]{2,1,0:T(8,128)S(1)} all-to-all(f32[8,16,128]{2,1,0:T(8,128)S(1)} %get-tuple-element.8), channel_id=1, replica_groups=mesh['scen'=8,'reach'=64] {'scen'}, dimensions={0} | all-to-all | bytes 131072 | tf_op jit(solution)/shard_map/all_to_all | solution.py:305
  55.0 24.2 %all_to_all.27.in_ref = f32[64,16,128]{2,1,0:T(8,128)S(1)} all-to-all(f32[64,16,128]{2,1,0:T(8,128)S(1)} %shard_map.72), channel_id=1, replica_groups=mesh['scen'=8,'reach'=64] {'reach'}, dimensions={0} | all-to-all | bytes 1048576 | tf_op jit(solution)/shard_map/all_to_all | solution.py:305
  79.3 0.1 shard_map.73
  79.4 11.2 %all_to_all.28.gram_ref = f32[8,16,128]{2,1,0:T(8,128)S(1)} all-to-all(f32[8,16,128]{2,1,0:T(8,128)S(1)} %shard_map.73), channel_id=1, replica_groups=mesh['scen'=8,'reach'=64] {'scen'}, dimensions={0} | all-to-all | bytes 131072 | tf_op jit(solution)/shard_map/all_to_all | solution.py:305
  90.5 5.7 %shard_map.74 = (f32[2,2048,128]{2,1,0:T(8,128)}, f32[128,128]{1,0:T(8,128)}) custom-call(f32[8,16,128]{2,1,0:T(8,128)S(1)} %all_to_all.28.gram_ref, bf16[2,128,2048]{2,1,0:T(8,128)(2,1)S(1)} %get-tuple-element.9.cols_ref), custom_call_target="tpu_custom_call" | custom-call | tf_op jit(solution)/shard_map/pallas_call | solution.py:361
  (2 shorter events, 0.1 us)
Async XLA Ops:
  19.0 23.5 %all-to-all-start.1 = ((f32[64,4,128]{2,1,0:T(4,128)}), f32[64,4,128]{2,1,0:T(4,128)S(1)}, u32[]{:S(2)}, u32[]{:S(2)}) async-start(f32[64,4,128]{2,1,0:T(4,128)} %get-tuple-element.7), calls=%async_computation.1 | async-start | bytes 262144 | tf_op jit(solution)/shard_map/all_to_all | solution.py:305
  31.0 1.7 %collective-permute-start = (f32[16,128]{1,0:T(8,128)S(1)}, f32[16,128]{1,0:T(8,128)S(1)}, u32[]{:S(2)}, u32[]{:S(2)}) collective-permute-start(f32[16,128]{1,0:T(8,128)S(1)} %shard_map.69), channel_id=1, source_target_pairs={{448,1},{449,2},{450,3},{451,4},{452,5},{453,6},{454,7},{455,8},{4... | collective-permute-start | bytes 24584 | tf_op jit(solution)/shard_map/ppermute | solution.py:343
  31.7 0.8 copy-start

commit v3 on v2

--- a/solution.py
+++ b/solution.py
@@ -12,6 +12,7 @@
 HALO = 16
 SCENS = 8
 REACHES = 64
+RING = 8
 COLS = SCENS * STEPS
 CELLS = 1048576
 PART = CELLS // REACHES
@@ -33,43 +34,49 @@
     return pltpu.CompilerParams(vmem_limit_bytes=mib * 1024 * 1024)
 
 
-def prepare_kernel(state_hbm, resist_hbm, flow_hbm, head_hbm, valve_hbm, edge_ref, out_ref, state, resist, flow, head, valve, sems):
-    loads = []
-    for which, (source, target) in enumerate(
-        ((resist_hbm, resist), (state_hbm, state), (flow_hbm, flow), (head_hbm, head), (valve_hbm, valve))
-    ):
-        copy = pltpu.make_async_copy(source, target, sems.at[which])
+def edges_kernel(state_hbm, resist_hbm, out_ref, ends, resist, sems):
+    rows = 2 * PART // LANES
+    loads = [
+        pltpu.make_async_copy(resist_hbm, resist, sems.at[0]),
+        pltpu.make_async_copy(state_hbm.at[pl.ds(0, 8), :], ends.at[0], sems.at[1]),
+        pltpu.make_async_copy(state_hbm.at[pl.ds(rows - 8, 8), :], ends.at[1], sems.at[2]),
+    ]
+    for copy in loads:
         copy.start()
-        loads.append(copy)
-    loads[0].wait()
+    for copy in loads:
+        copy.wait()
     lane = lax.broadcasted_iota(jnp.int32, (1, LANES), 1)
     total = jnp.sum(jnp.sum(resist[...], axis=0, keepdims=True), axis=1, keepdims=True)
-    ends = jnp.where(
-        lane < HALO, resist[0:1, :], jnp.where(lane >= LANES - HALO, resist[LANES - 1 : LANES, :], 0.0)
-    )
-    upto = ends
+
+    def both(first, final):
+        return jnp.where(lane < HALO, first, jnp.where(lane >= LANES - HALO, final, 0.0))
+
+    outer = both(resist[0:1, :], resist[LANES - 1 : LANES, :])
+    upto = outer
     for step in (1, 2, 4, 8):
         upto = upto + jnp.where(lane >= step, pltpu.roll(upto, step, 1), 0.0)
     upto = jnp.where(lane < HALO, upto, upto - upto[:, LANES - 1 : LANES])
-    row = jnp.concatenate([ends, upto, jnp.broadcast_to(total, (1, LANES)), ends], axis=0)
-    edge_ref[...] = jnp.broadcast_to(row[None], (REACHES, 4, LANES))
-    for copy in loads[1:]:
-        copy.wait()
+    upto = jnp.where((lane >= HALO) & (lane < LANES - HALO), total, upto)
+    row = jnp.concatenate(
+        [both(ends[0, 0:1, :], ends[1, 6:7, :]), both(ends[0, 1:2, :], ends[1, 7:8, :]), outer, upto], axis=0
+    )
+    out_ref[...] = jnp.broadcast_to(row[None], (REACHES, 4, LANES))
+
+
+def window_kernel(state_ref, resist_ref, flow_ref, head_ref, valve_ref, out_ref, aux_ref):
     rows = 2 * BLOCKS
     none = jnp.zeros((2, LANES), jnp.float32)
     for which in range(SCENS):
         start = which * rows
-        out_ref[which, 0:rows, :] = state[start : start + rows, :]
-        after = state[start + rows : start + rows + 2, :] if which < SCENS - 1 else none
+        out_ref[which, 0:rows, :] = state_ref[start : start + rows, :]
+        after = state_ref[start + rows : start + rows + 2, :] if which < SCENS - 1 else none
         out_ref[which, RIGHT_ROW : RIGHT_ROW + 2, :] = after
-        out_ref[which, LEFT_ROW : LEFT_ROW + 2, :] = state[start - 2 : start, :] if which > 0 else none
+        out_ref[which, LEFT_ROW : LEFT_ROW + 2, :] = state_ref[start - 2 : start, :] if which > 0 else none
         out_ref[which, HEAD_ROW:WINDOW, :] = jnp.zeros((WINDOW - HEAD_ROW, LANES), jnp.float32)
-        out_ref[which, HEAD_ROW : HEAD_ROW + 1, 0:STEPS] = head[...]
-        out_ref[which, VALVE_ROW : VALVE_ROW + 1, 0:STEPS] = valve[...]
-        out_ref[which, FLOW_ROW : FLOW_ROW + 1, :] = jnp.full((1, LANES), flow[0], jnp.float32)
-
-
-def spread_kernel(resist_ref, aux_ref):
+        out_ref[which, HEAD_ROW : HEAD_ROW + 1, 0:STEPS] = head_ref[...]
+        out_ref[which, VALVE_ROW : VALVE_ROW + 1, 0:STEPS] = valve_ref[...]
+        out_ref[which, FLOW_ROW : FLOW_ROW + 1, :] = jnp.full((1, LANES), flow_ref[0], jnp.float32)
+
     scen = lax.axis_index("scen")
     first = scen * BLOCKS
     row_left = resist_ref[pl.ds(jnp.maximum(first - 1, 0), 1), :]
@@ -98,15 +105,13 @@
     aux_ref[24:48, :] = base + (shift + inside)
 
 
-def outer_kernel(win_ref, out_ref):
-    low = lax.axis_index("scen") == 0
-    for field in range(2):
-        first = win_ref[pl.ds(field, SCENS, stride=WINDOW), :]
-        final = win_ref[pl.ds(RIGHT_ROW - 2 + field, SCENS, stride=WINDOW), :]
-        out_ref[field * SCENS : (field + 1) * SCENS, :] = jnp.where(low, first, final)
-
-
-def step_kernel(win_ref, outer_ref, edge_ref, aux_ref, cols_ref, gram_ref, wide_ref, plan_ref, kept_ref):
+def patch_kernel(win_ref, edge_ref, out_ref):
+    reach = lax.axis_index("reach")
+    out_ref[0, LEFT_ROW : LEFT_ROW + 2, :] = edge_ref[jnp.maximum(reach - 1, 0), 0:2, :]
+    out_ref[SCENS - 1, RIGHT_ROW : RIGHT_ROW + 2, :] = edge_ref[jnp.minimum(reach + 1, REACHES - 1), 0:2, :]
+
+
+def step_kernel(win_ref, edge_ref, aux_ref, cols_ref, gram_ref, wide_ref, plan_ref, kept_ref):
     scen = lax.axis_index("scen")
     reach = lax.axis_index("reach")
     lane = lax.broadcasted_iota(jnp.int32, (SCENS, LANES), 1)
@@ -132,9 +137,10 @@
     mean_flow = steady * CELLS ** (-0.5)
     first_head = plan_ref[0, 0:SCENS, :]
     place = lax.broadcasted_iota(jnp.int32, (REACHES, 1), 0)
-    totals = edge_ref[:, 2, :]
-    upstream = jnp.sum(jnp.where(place < reach, totals, 0.0), axis=0, keepdims=True)
-    through = jnp.sum(jnp.where(place <= reach, totals, 0.0), axis=0, keepdims=True)
+    totals = edge_ref[:, 3, :]
+    middle = slice(LANES // 2, LANES // 2 + 1)
+    upstream = jnp.sum(jnp.where(place < reach, totals, 0.0), axis=0, keepdims=True)[:, middle]
+    through = jnp.sum(jnp.where(place <= reach, totals, 0.0), axis=0, keepdims=True)[:, middle]
     previous = edge_ref[jnp.maximum(reach - 1, 0)]
     following = edge_ref[jnp.minimum(reach + 1, REACHES - 1)]
     none = jnp.zeros((SCENS, LANES), jnp.float32)
@@ -148,10 +154,8 @@
             beyond, edge, base = (
                 (scen == 0, previous, upstream) if j == 0 else (scen == SCENS - 1, following, through)
             )
-            resist = jnp.where(beyond, edge[0:1], resist)
-            running = jnp.where(beyond, base + edge[1:2], running)
-            head = jnp.where(beyond, outer_ref[0:SCENS, :], head)
-            flow = jnp.where(beyond, outer_ref[SCENS:, :], flow)
+            resist = jnp.where(beyond, edge[2:3], resist)
+            running = jnp.where(beyond, base + edge[3:4], running)
         wide_ref[0, j] = first_head - running * scale + head
         wide_ref[1, j] = mean_flow + flow
         for state in range(4):
@@ -301,46 +305,49 @@
     )(value)
 
 
-def exchanged(value, axis):
-    return lax.all_to_all(value, axis, split_axis=0, concat_axis=0, tiled=True)
+def exchanged(value, axis, groups=None):
+    return lax.all_to_all(value, axis, split_axis=0, concat_axis=0, axis_index_groups=groups, tiled=True)
 
 
 def local(perturb, resist, flow_rate, head_plan, valve_plan):
     f32 = jnp.float32
     vmem = pl.BlockSpec(memory_space=pltpu.VMEM)
+    smem = pl.BlockSpec(memory_space=pltpu.SMEM)
     hbm = pl.BlockSpec(memory_space=pltpu.HBM)
     blocks = PART // LANES
     state = perturb.reshape(2, blocks, LANES).transpose(1, 0, 2).reshape(2 * blocks, LANES)
     resist = resist.reshape(LANES, LANES)
-    edges, windows = pl.pallas_call(
-        prepare_kernel,
-        in_specs=[hbm] * 5,
-        out_specs=(vmem, vmem),
+    edges = pl.pallas_call(
+        edges_kernel,
+        in_specs=[hbm, hbm],
+        out_specs=vmem,
+        out_shape=jax.ShapeDtypeStruct((REACHES, 4, LANES), f32),
+        scratch_shapes=[
+            pltpu.VMEM((2, 8, LANES), f32),
+            pltpu.VMEM((LANES, LANES), f32),
+            pltpu.SemaphoreType.DMA((3,)),
+        ],
+        compiler_params=params(61),
+    )(state, resist)
+    edges = exchanged(edges, "reach")
+    windows, aux = pl.pallas_call(
+        window_kernel,
+        in_specs=[vmem, vmem, smem, vmem, vmem],
         out_shape=(
-            jax.ShapeDtypeStruct((REACHES, 4, LANES), f32),
             jax.ShapeDtypeStruct((SCENS, WINDOW, LANES), f32),
+            jax.ShapeDtypeStruct((48, LANES), f32),
         ),
-        scratch_shapes=[
-            pltpu.VMEM((2 * blocks, LANES), f32),
-            pltpu.VMEM((LANES, LANES), f32),
-            pltpu.SMEM((1,), f32),
-            pltpu.VMEM((1, STEPS), f32),
-            pltpu.VMEM((1, STEPS), f32),
-            pltpu.SemaphoreType.DMA((5,)),
-        ],
-        compiler_params=params(60),
+        compiler_params=params(),
     )(state, resist, flow_rate, head_plan, valve_plan)
-    edges = exchanged(edges, "reach")
-    aux = pl.pallas_call(
-        spread_kernel, out_shape=jax.ShapeDtypeStruct((48, LANES), f32), compiler_params=params()
-    )(resist)
+    windows = pl.pallas_call(
+        patch_kernel,
+        in_specs=[vmem, vmem],
+        out_specs=vmem,
+        out_shape=jax.ShapeDtypeStruct((SCENS, WINDOW, LANES), f32),
+        input_output_aliases={0: 0},
+        compiler_params=params(),
+    )(windows, edges)
     windows = exchanged(windows, "scen").reshape(SCENS * WINDOW, LANES)
-    outer = pl.pallas_call(
-        outer_kernel, out_shape=jax.ShapeDtypeStruct((2 * SCENS, LANES), f32), compiler_params=params()
-    )(windows)
-    top = (SCENS - 1) * REACHES
-    pairs = [(top + r, r + 1) for r in range(REACHES - 1)]
-    outer = lax.ppermute(outer, ("scen", "reach"), pairs + [(b, a) for a, b in pairs])
     columns, gram = pl.pallas_call(
         step_kernel,
         out_shape=(
@@ -353,9 +360,12 @@
             pltpu.VMEM((2, BLOCKS, COLS, LANES), f32),
         ],
         compiler_params=params(),
-    )(windows, outer, edges, aux)
-    gram = fold(exchanged(gram, "scen"), REACHES)
-    gram = fold(exchanged(gram, "reach"), SCENS)
+    )(windows, edges, aux)
+    along = [[RING * a + b for b in range(RING)] for a in range(RING)]
+    across = [[RING * b + a for b in range(RING)] for a in range(RING)]
+    gram = fold(exchanged(gram, "scen"), RING)
+    gram = fold(exchanged(gram, "reach", along), RING)
+    gram = fold(exchanged(gram, "reach", across), SCENS)
     gram = exchanged(gram, "scen")
     chunks = 2 * SHARE // CHUNK
     return pl.pallas_call(

time: 96.7 us -> 89.9 us (0.930)
  blocking collectives: 60.6 us -> 49.5 us
  starting transfers between devices: 12.6 us -> 17.1 us
  waiting for transfers between devices: 9.82 us -> 7.56 us
  local copies, waits for them, and re-layouts: 0.83 us -> 3.05 us
    all_to_all x4 -> x5, blocking collectives: 60.6 us -> 49.5 us  [exchanged(): lax.all_to_all(value, axis, split_axis=0, concat_axis=0, axis_index_group...]
    all_to_all x1, starting transfers between devices: 11.9 us -> 17.1 us  [exchanged(): lax.all_to_all(value, axis, split_axis=0, concat_axis=0, axis_index_group...]
    all_to_all x1, waiting for transfers between devices: 9.82 us -> 7.56 us  [exchanged(): lax.all_to_all(value, axis, split_axis=0, concat_axis=0, axis_index_group...]
    unnamed x2 -> x8, local copies, waits for them, and re-layouts: 0.83 us -> 3.05 us
  transfers between devices with their start and end apart: 2 -> 1, of which waited for: 1 -> 1; matrix products, arithmetic and copies ran while one was open for 0% -> 0% of each run, Pallas kernels for 0% -> 0%
where the time goes in v3:
time: 89.9 us; the launch traced here: 89.4 us
  blocking collectives  49.5 us (55%)
  starting transfers between devices  17.1 us (19%)
  Pallas kernels  10.9 us (12%)
  waiting for transfers between devices  7.56 us (8%)
  local copies, waits for them, and re-layouts  3.05 us (3%)
  between operations  1.33 us (1%)
    all_to_all x5, blocking collectives, exchanged(): lax.all_to_all(value, axis, split_axis=0, concat_axis=0, axis_index_group...  49.5 us
    all_to_all x1, starting transfers between devices, exchanged(): lax.all_to_all(value, axis, split_axis=0, concat_axis=0, axis_index_group...  17.1 us
    all_to_all x1, waiting for transfers between devices, exchanged(): lax.all_to_all(value, axis, split_axis=0, concat_axis=0, axis_index_group...  7.56 us
    pallas_call x1, Pallas kernels, local(): pl.pallas_call(basis_kernel, in_specs=[vmem, vmem], out_specs=(pl.BlockSp...  5.71 us
    unnamed x8, local copies, waits for them, and re-layouts  3.05 us
    pallas_call x1, Pallas kernels, local(): pl.pallas_call(step_kernel, out_shape=(jax.ShapeDtypeStruct((2, COLS, SHA...  3.02 us
    pallas_call x1, Pallas kernels, local(): pl.pallas_call(edges_kernel, in_specs=[hbm, hbm], out_specs=vmem, out_sha...  1.89 us
  transfers between devices with their start and end apart: 1, of which 1 were waited for; matrix products, arithmetic and copies ran while one was open for 0% of the time, Pallas kernels for 0%

profile of v3, /device:TPU:1, one launch (start us, length us, event | category | flops | bytes accessed | tf_op | source)
XLA Modules:
  0.0 89.4 jit_solution(15077500540867357684)
XLA Ops:
  0.6 1.9 %shard_map.69 = f32[64,4,128]{2,1,0:T(4,128)} custom-call(f32[256,128]{1,0:T(8,128)} %bitcast.8, f32[128,128]{1,0:T(8,128)} %bitcast.10), custom_call_target="tpu_custom_call" | custom-call | tf_op jit(solution)/shard_map/pallas_call | solution.py:320
  2.5 17.1 %all-to-all-start = ((f32[64,4,128]{2,1,0:T(4,128)}), f32[64,4,128]{2,1,0:T(4,128)S(1)}, u32[]{:S(2)}, u32[]{:S(2)}) async-start(f32[64,4,128]{2,1,0:T(4,128)} %shard_map.69), calls=%async_computation | async-start | bytes 262144 | tf_op jit(solution)/shard_map/all_to_all | solution.py:309
  20.3 0.0 copy-start
  20.3 0.9 %copy-done = f32[1,2,16384]{2,1,0:T(2,128)S(1)} copy-done((f32[1,2,16384]{2,1,0:T(2,128)S(1)}, f32[1,2,16384]{2,1,0:T(2,128)}, u32[]{:S(2)}) %copy-start) | copy-done | bytes 131096
  21.2 0.0 copy-start.1
  21.2 0.8 copy-done.1
  22.1 0.0 copy-start.2
  22.1 0.7 copy-done.2
  22.7 0.0 copy-start.3
  22.7 0.7 copy-done.3
  23.4 0.2 shard_map.68
  23.6 7.6 %all-to-all-done.edge_ref = f32[64,4,128]{2,1,0:T(4,128)S(1)} async-done(((f32[64,4,128]{2,1,0:T(4,128)}), f32[64,4,128]{2,1,0:T(4,128)S(1)}, u32[]{:S(2)}, u32[]{:S(2)}) %all-to-all-start) | async-done | bytes 131104 | tf_op jit(solution)/shard_map/all_to_all | solution.py:309
  31.2 11.8 %all_to_all.30 = f32[8,40,128]{2,1,0:T(8,128)S(1)} all-to-all(f32[8,40,128]{2,1,0:T(8,128)S(1)} %shard_map.70), channel_id=1, replica_groups=mesh['scen'=8,'reach'=64] {'scen'}, dimensions={0} | all-to-all | bytes 327680 | tf_op jit(solution)/shard_map/all_to_all | solution.py:309
  43.0 3.0 %shard_map.71 = (bf16[2,128,2048]{2,1,0:T(8,128)(2,1)S(1)}, f32[8,16,128]{2,1,0:T(8,128)S(1)}) custom-call(f32[320,128]{1,0:T(8,128)S(1)} %bitcast.7, f32[64,4,128]{2,1,0:T(4,128)S(1)} %all-to-all-done.edge_ref, f32[48,128]{1,0:T(8,128)S(1)} %get-tuple-element.7.aux_ref), custom_call_target="tpu_custom_call" | custom-call | tf_op jit(solution)/shard_map/pallas_call | solution.py:351
  46.0 8.1 %all_to_all.31.in_ref = f32[8,16,128]{2,1,0:T(8,128)S(1)} all-to-all(f32[8,16,128]{2,1,0:T(8,128)S(1)} %get-tuple-element.8), channel_id=1, replica_groups=mesh['scen'=8,'reach'=64] {'scen'}, dimensions={0} | all-to-all | bytes 131072 | tf_op jit(solution)/shard_map/all_to_all | solution.py:309
  54.2 9.7 %all_to_all.32.in_ref = f32[8,16,128]{2,1,0:T(8,128)S(1)} all-to-all(f32[8,16,128]{2,1,0:T(8,128)S(1)} %shard_map.72), channel_id=1, replica_groups={{0,1,2,3,4,5,6,7},{8,9,10,11,12,13,14,15},{16,17,18,19,20,21,22,23},{24..., dimensions={0} | all-to-all | bytes 131072 | tf_op jit(solution)/shard_map/all_to_all | solution.py:309
  63.9 9.7 %all_to_all.33.in_ref = f32[8,16,128]{2,1,0:T(8,128)S(1)} all-to-all(f32[8,16,128]{2,1,0:T(8,128)S(1)} %shard_map.73), channel_id=1, replica_groups={{0,8,16,24,32,40,48,56},{1,9,17,25,33,41,49,57},{2,10,18,26,34,42,50,58..., dimensions={0} | all-to-all | bytes 131072 | tf_op jit(solution)/shard_map/all_to_all | solution.py:309
  73.6 10.1 %all_to_all.34.gram_ref = f32[8,16,128]{2,1,0:T(8,128)S(1)} all-to-all(f32[8,16,128]{2,1,0:T(8,128)S(1)} %shard_map.74), channel_id=1, replica_groups=mesh['scen'=8,'reach'=64] {'scen'}, dimensions={0} | all-to-all | bytes 131072 | tf_op jit(solution)/shard_map/all_to_all | solution.py:309
  83.7 5.7 %shard_map.75 = (f32[2,2048,128]{2,1,0:T(8,128)}, f32[128,128]{1,0:T(8,128)}) custom-call(f32[8,16,128]{2,1,0:T(8,128)S(1)} %all_to_all.34.gram_ref, bf16[2,128,2048]{2,1,0:T(8,128)(2,1)S(1)} %get-tuple-element.9.cols_ref), custom_call_target="tpu_custom_call" | custom-call | tf_op jit(solution)/shard_map/pallas_call | solution.py:371
  (4 shorter events, 0.0 us)
Async XLA Ops:
  2.5 28.7 %all-to-all-start = ((f32[64,4,128]{2,1,0:T(4,128)}), f32[64,4,128]{2,1,0:T(4,128)S(1)}, u32[]{:S(2)}, u32[]{:S(2)}) async-start(f32[64,4,128]{2,1,0:T(4,128)} %shard_map.69), calls=%async_computation | async-start | bytes 262144 | tf_op jit(solution)/shard_map/all_to_all | solution.py:309
  20.3 0.9 %copy-start = (f32[1,2,16384]{2,1,0:T(2,128)S(1)}, f32[1,2,16384]{2,1,0:T(2,128)}, u32[]{:S(2)}) copy-start(f32[1,2,16384]{2,1,0:T(2,128)} %param.5) | copy-start | bytes 393220
  21.2 0.8 copy-start.1
  22.1 0.7 copy-start.2
  22.7 0.7 copy-start.3

commit v4 on v3

--- a/solution.py
+++ b/solution.py
@@ -27,6 +27,9 @@
 WIDE = BLOCKS + 2
 PANEL = 64
 CHUNK = 256
+HALF = COLS // 2
+QUARTER = COLS // 4
+PIECES = 3
 EXACT = lax.Precision.HIGHEST
 
 
@@ -46,21 +49,34 @@
     for copy in loads:
         copy.wait()
     lane = lax.broadcasted_iota(jnp.int32, (1, LANES), 1)
+    is_first, is_final = lane < HALO, lane >= LANES - HALO
     total = jnp.sum(jnp.sum(resist[...], axis=0, keepdims=True), axis=1, keepdims=True)
-
-    def both(first, final):
-        return jnp.where(lane < HALO, first, jnp.where(lane >= LANES - HALO, final, 0.0))
-
-    outer = both(resist[0:1, :], resist[LANES - 1 : LANES, :])
+    outer = jnp.where(is_first, resist[0:1, :], jnp.where(is_final, resist[LANES - 1 : LANES, :], 0.0))
     upto = outer
     for step in (1, 2, 4, 8):
         upto = upto + jnp.where(lane >= step, pltpu.roll(upto, step, 1), 0.0)
-    upto = jnp.where(lane < HALO, upto, upto - upto[:, LANES - 1 : LANES])
-    upto = jnp.where((lane >= HALO) & (lane < LANES - HALO), total, upto)
-    row = jnp.concatenate(
-        [both(ends[0, 0:1, :], ends[1, 6:7, :]), both(ends[0, 1:2, :], ends[1, 7:8, :]), outer, upto], axis=0
-    )
-    out_ref[...] = jnp.broadcast_to(row[None], (REACHES, 4, LANES))
+    back = jnp.where(lane == LANES - 1, total, upto - upto[:, LANES - 1 : LANES])
+    firsts = (ends[0, 0:1, :], ends[0, 1:2, :], resist[0:1, :], upto)
+    finals = (ends[1, 6:7, :], ends[1, 7:8, :], resist[LANES - 1 : LANES, :], back)
+    row = jnp.zeros((1, LANES), jnp.float32)
+    for place, (first, final) in enumerate(zip(firsts, finals)):
+        low, high = jnp.where(is_first, first, 0.0), jnp.where(is_final, final, 0.0)
+        if place:
+            low, high = pltpu.roll(low, place * HALO, 1), pltpu.roll(high, LANES - place * HALO, 1)
+        row = row + low + high
+    out_ref[...] = jnp.broadcast_to(row[None], (REACHES, 1, LANES))
+
+
+def last_of(row, place):
+    lane = lax.broadcasted_iota(jnp.int32, (1, LANES), 1)
+    moved = pltpu.roll(row, place * HALO, 1) if place else row
+    return jnp.where(lane >= LANES - HALO, moved, 0.0)
+
+
+def first_of(row, place):
+    lane = lax.broadcasted_iota(jnp.int32, (1, LANES), 1)
+    moved = pltpu.roll(row, LANES - place * HALO, 1) if place else row
+    return jnp.where(lane < HALO, moved, 0.0)
 
 
 def window_kernel(state_ref, resist_ref, flow_ref, head_ref, valve_ref, out_ref, aux_ref):
@@ -107,11 +123,14 @@
 
 def patch_kernel(win_ref, edge_ref, out_ref):
     reach = lax.axis_index("reach")
-    out_ref[0, LEFT_ROW : LEFT_ROW + 2, :] = edge_ref[jnp.maximum(reach - 1, 0), 0:2, :]
-    out_ref[SCENS - 1, RIGHT_ROW : RIGHT_ROW + 2, :] = edge_ref[jnp.minimum(reach + 1, REACHES - 1), 0:2, :]
-
-
-def step_kernel(win_ref, edge_ref, aux_ref, cols_ref, gram_ref, wide_ref, plan_ref, kept_ref):
+    previous = edge_ref[jnp.maximum(reach - 1, 0)]
+    following = edge_ref[jnp.minimum(reach + 1, REACHES - 1)]
+    for field in range(2):
+        out_ref[0, LEFT_ROW + field : LEFT_ROW + field + 1, :] = last_of(previous, field)
+        out_ref[SCENS - 1, RIGHT_ROW + field : RIGHT_ROW + field + 1, :] = first_of(following, field)
+
+
+def step_kernel(win_ref, edge_ref, aux_ref, cols_ref, gram_ref, wide_ref, plan_ref, kept_ref, order_ref):
     scen = lax.axis_index("scen")
     reach = lax.axis_index("reach")
     lane = lax.broadcasted_iota(jnp.int32, (SCENS, LANES), 1)
@@ -136,11 +155,11 @@
     scale = steady * jnp.abs(steady) * (1.0 / CELLS)
     mean_flow = steady * CELLS ** (-0.5)
     first_head = plan_ref[0, 0:SCENS, :]
-    place = lax.broadcasted_iota(jnp.int32, (REACHES, 1), 0)
-    totals = edge_ref[:, 3, :]
-    middle = slice(LANES // 2, LANES // 2 + 1)
-    upstream = jnp.sum(jnp.where(place < reach, totals, 0.0), axis=0, keepdims=True)[:, middle]
-    through = jnp.sum(jnp.where(place <= reach, totals, 0.0), axis=0, keepdims=True)[:, middle]
+    place = lax.broadcasted_iota(jnp.int32, (REACHES, 1, LANES), 0)
+    held = edge_ref[...]
+    at_total = slice(LANES - 3 * HALO - 1, LANES - 3 * HALO)
+    upstream = jnp.sum(jnp.where(place < reach, held, 0.0), axis=0)[:, at_total]
+    through = jnp.sum(jnp.where(place <= reach, held, 0.0), axis=0)[:, at_total]
     previous = edge_ref[jnp.maximum(reach - 1, 0)]
     following = edge_ref[jnp.minimum(reach + 1, REACHES - 1)]
     none = jnp.zeros((SCENS, LANES), jnp.float32)
@@ -151,72 +170,88 @@
         running = upstream + aux_ref[24 + at : 25 + at, :]
         head, flow = taken(row), taken(row + 1)
         if j in (0, WIDE - 1):
-            beyond, edge, base = (
-                (scen == 0, previous, upstream) if j == 0 else (scen == SCENS - 1, following, through)
-            )
-            resist = jnp.where(beyond, edge[2:3], resist)
-            running = jnp.where(beyond, base + edge[3:4], running)
+            if j == 0:
+                beyond, base = scen == 0, upstream
+                edge, upto = last_of(previous, 2), last_of(previous, 3)
+                upto = jnp.where(is_high[0:1], 0.0, upto)
+            else:
+                beyond, base = scen == SCENS - 1, through
+                edge, upto = first_of(following, 2), first_of(following, 3)
+            resist = jnp.where(beyond, edge, resist)
+            running = jnp.where(beyond, base + upto, running)
         wide_ref[0, j] = first_head - running * scale + head
         wide_ref[1, j] = mean_flow + flow
         for state in range(4):
             wide_ref[2 + state, j] = none
         wide_ref[6, j] = jnp.broadcast_to(resist, (SCENS, LANES))
 
-    def one_step(moment, carry):
-        plan_rows = pl.ds(pl.multiple_of(moment * SCENS, SCENS), SCENS)
-        head_left = plan_ref[0, plan_rows, :]
-        small = plan_ref[1, plan_rows, :]
-        large = plan_ref[2, plan_rows, :]
-
-        def sent(j):
-            head, flow = wide_ref[0, j], wide_ref[1, j]
-            friction = wide_ref[6, j] * flow * jnp.abs(flow) + (
-                (wide_ref[2, j] + wide_ref[3, j]) + (wide_ref[4, j] + wide_ref[5, j])
-            )
-            net = flow - friction
-            return pltpu.roll(head + net, 1, 1), pltpu.roll(head - net, LANES - 1, 1)
-
-        forward_before, (forward, backward) = None, sent(0)
-        for j in range(WIDE):
-            forward_after, backward_after = sent(j + 1) if j + 1 < WIDE else (forward, backward)
-            if forward_before is None:
-                forward_before = forward
-            from_left = jnp.where(is_low, forward_before, forward)
-            from_right = jnp.where(is_high, backward_after, backward)
-            new_head = 0.5 * (from_left + from_right)
-            new_flow = 0.5 * (from_left - from_right)
-            if j == 1:
-                new_head = jnp.where(at_first, head_left, new_head)
-                new_flow = jnp.where(at_first, head_left - from_right, new_flow)
-            if j == BLOCKS:
-                new_head = jnp.where(at_last, from_left * small, new_head)
-                new_flow = jnp.where(at_last, from_left * large, new_flow)
-            change = new_flow - wide_ref[1, j]
-            wide_ref[0, j] = new_head
-            wide_ref[1, j] = new_flow
-            for state in range(4):
-                wide_ref[2 + state, j] = RETAINS[state] * wide_ref[2 + state, j] + SHARES[state] * change
-            if 1 <= j <= BLOCKS:
-                kept_ref[0, j - 1, plan_rows, :] = new_head
-                kept_ref[1, j - 1, plan_rows, :] = new_flow
-            forward_before, forward, backward = forward, forward_after, backward_after
+    def two_steps(pair, carry):
+        for half in range(2):
+            plan_rows = pl.ds(pl.multiple_of((2 * pair + half) * SCENS, SCENS), SCENS)
+            head_left = plan_ref[0, plan_rows, :]
+            small = plan_ref[1, plan_rows, :]
+            large = plan_ref[2, plan_rows, :]
+
+            def sent(j):
+                head, flow = wide_ref[0, j], wide_ref[1, j]
+                friction = wide_ref[6, j] * flow * jnp.abs(flow) + (
+                    (wide_ref[2, j] + wide_ref[3, j]) + (wide_ref[4, j] + wide_ref[5, j])
+                )
+                net = flow - friction
+                return pltpu.roll(head + net, 1, 1), pltpu.roll(head - net, LANES - 1, 1)
+
+            forward_before, (forward, backward) = None, sent(0)
+            for j in range(WIDE):
+                forward_after, backward_after = sent(j + 1) if j + 1 < WIDE else (forward, backward)
+                if forward_before is None:
+                    forward_before = forward
+                from_left = jnp.where(is_low, forward_before, forward)
+                from_right = jnp.where(is_high, backward_after, backward)
+                new_head = 0.5 * (from_left + from_right)
+                new_flow = 0.5 * (from_left - from_right)
+                if j == 1:
+                    new_head = jnp.where(at_first, head_left, new_head)
+                    new_flow = jnp.where(at_first, head_left - from_right, new_flow)
+                if j == BLOCKS:
+                    new_head = jnp.where(at_last, from_left * small, new_head)
+                    new_flow = jnp.where(at_last, from_left * large, new_flow)
+                change = new_flow - wide_ref[1, j]
+                wide_ref[0, j] = new_head
+                wide_ref[1, j] = new_flow
+                for state in range(4):
+                    wide_ref[2 + state, j] = RETAINS[state] * wide_ref[2 + state, j] + SHARES[state] * change
+                if 1 <= j <= BLOCKS:
+                    for field, value in enumerate((new_head, new_flow)):
+                        if half == 0:
+                            kept_ref[field, j - 1] = value
+                        else:
+                            both = jnp.concatenate([kept_ref[field, j - 1], value], axis=0)
+                            cols_ref[
+                                field,
+                                pl.ds(pl.multiple_of(pair * 2 * SCENS, 2 * SCENS), 2 * SCENS),
+                                (j - 1) * LANES : j * LANES,
+                            ] = both.astype(jnp.bfloat16)
+                forward_before, forward, backward = forward, forward_after, backward_after
         return carry
 
-    lax.fori_loop(0, STEPS, one_step, 0)
-
-    for field in range(2):
-        for j in range(BLOCKS):
-            for which in range(SCENS):
-                piece = kept_ref[field, j, pl.ds(which, STEPS, stride=SCENS), :]
-                cols_ref[field, which * STEPS : (which + 1) * STEPS, j * LANES : (j + 1) * LANES] = piece.astype(
-                    jnp.bfloat16
-                )
+    lax.fori_loop(0, STEPS // 2, two_steps, 0)
+
     total = None
     for field in range(2):
         columns = cols_ref[field]
         part = lax.dot_general(columns, columns, (((1,), (1,)), ((), ())), preferred_element_type=jnp.float32)
         total = part if total is None else total + part
-    gram_ref[...] = total.reshape(SCENS, STEPS, COLS)
+    order_ref[...] = total
+    rows = [order_ref[pl.ds(which, STEPS, stride=SCENS), :] for which in range(SCENS)]
+    order_ref[...] = jnp.concatenate(rows, axis=0).T
+    rows = [order_ref[pl.ds(which, STEPS, stride=SCENS), :] for which in range(SCENS)]
+    high = lax.broadcasted_iota(jnp.int32, (QUARTER, COLS), 1) >= HALF
+    upper, lower = jnp.concatenate(rows[4:6], axis=0), jnp.concatenate(rows[6:8], axis=0)
+    packed = jnp.concatenate(rows[0:4] + [jnp.where(high, upper, pltpu.roll(lower, HALF, 1))], axis=0)
+    for which in range(SCENS):
+        for part in range(PIECES):
+            at = (which * PIECES + part) * 4
+            gram_ref[which, part] = packed[at : at + 4, :]
 
 
 def fold_kernel(in_ref, out_ref):
@@ -228,12 +263,19 @@
         out_ref[which] = total
 
 
-def basis_kernel(gram_ref, cols_ref, rows_ref, tri_ref, work_ref, out_ref, sems):
+def basis_kernel(gram_ref, cols_ref, rows_ref, tri_ref, work_ref, turned_ref, order_ref, out_ref, sems):
     scale = 1.0 / (2 * CELLS)
     sub = lax.broadcasted_iota(jnp.int32, (8, COLS), 0)
     lane = lax.broadcasted_iota(jnp.int32, (8, COLS), 1)
     groups = PANEL // 8
-    work_ref[:, 0:COLS] = gram_ref[...].reshape(COLS, COLS) * scale
+    for field in range(2):
+        for part in range(SHARE // CHUNK):
+            turned_ref[field * (SHARE // CHUNK) + part] = cols_ref[field, :, part * CHUNK : (part + 1) * CHUNK].T
+    for which in range(SCENS):
+        for part in range(PIECES):
+            at = (which * PIECES + part) * 4
+            work_ref[at : at + 4, 0:COLS] = gram_ref[which, part] * scale
+    work_ref[HALF + QUARTER :, 0:COLS] = pltpu.roll(work_ref[HALF : HALF + QUARTER, 0:COLS], HALF, 1)
     for g in range(COLS // 8):
         work_ref[8 * g : 8 * g + 8, COLS:] = jnp.where(lane == sub + 8 * g, 1.0, 0.0).astype(jnp.float32)
     inverse_rows = []
@@ -275,7 +317,8 @@
                 preferred_element_type=jnp.float32,
             )
             work_ref[low + PANEL :, :] = work_ref[low + PANEL :, :] - update[low + PANEL :, :]
-    inverse = jnp.concatenate(inverse_rows, axis=0).T
+    order_ref[...] = jnp.concatenate(inverse_rows, axis=0).T
+    inverse = jnp.concatenate([order_ref[pl.ds(n, SCENS, stride=STEPS), :] for n in range(STEPS)], axis=0)
     high = inverse.astype(jnp.bfloat16)
     rest = inverse - high.astype(jnp.float32)
     middle = rest.astype(jnp.bfloat16)
@@ -283,8 +326,8 @@
     copies = []
     for field in range(2):
         for part in range(SHARE // CHUNK):
-            piece = cols_ref[field, :, part * CHUNK : (part + 1) * CHUNK].T
             slot = len(copies)
+            piece = turned_ref[slot]
             out_ref[slot] = jnp.dot(
                 jnp.concatenate([piece, piece], axis=1), both, preferred_element_type=jnp.float32
             )
@@ -321,7 +364,7 @@
         edges_kernel,
         in_specs=[hbm, hbm],
         out_specs=vmem,
-        out_shape=jax.ShapeDtypeStruct((REACHES, 4, LANES), f32),
+        out_shape=jax.ShapeDtypeStruct((REACHES, 1, LANES), f32),
         scratch_shapes=[
             pltpu.VMEM((2, 8, LANES), f32),
             pltpu.VMEM((LANES, LANES), f32),
@@ -352,12 +395,13 @@
         step_kernel,
         out_shape=(
             jax.ShapeDtypeStruct((2, COLS, SHARE), jnp.bfloat16),
-            jax.ShapeDtypeStruct((SCENS, STEPS, COLS), f32),
+            jax.ShapeDtypeStruct((SCENS, PIECES, 4, COLS), f32),
         ),
         scratch_shapes=[
             pltpu.VMEM((7, WIDE, SCENS, LANES), f32),
             pltpu.VMEM((3, STEPS * SCENS, LANES), f32),
-            pltpu.VMEM((2, BLOCKS, COLS, LANES), f32),
+            pltpu.VMEM((2, BLOCKS, SCENS, LANES), f32),
+            pltpu.VMEM((COLS, COLS), f32),
         ],
         compiler_params=params(),
     )(windows, edges, aux)
@@ -378,6 +422,8 @@
         ),
         scratch_shapes=[
             pltpu.VMEM((COLS, 2 * COLS), f32),
+            pltpu.VMEM((chunks, CHUNK, COLS), jnp.bfloat16),
+            pltpu.VMEM((COLS, COLS), f32),
             pltpu.VMEM((chunks, CHUNK, COLS), f32),
             pltpu.SemaphoreType.DMA((chunks,)),
         ],

time: 89.9 us -> 89 us (0.990)
  no operation moved by 1% of the time
where the time goes in v4:
time: 89 us; the launch traced here: 88.5 us
  blocking collectives  49.3 us (55%)
  starting transfers between devices  17.1 us (19%)
  Pallas kernels  10.9 us (12%)
  waiting for transfers between devices  6.83 us (8%)
  local copies, waits for them, and re-layouts  3.05 us (3%)
  between operations  1.32 us (1%)
    all_to_all x5, blocking collectives, exchanged(): lax.all_to_all(value, axis, split_axis=0, concat_axis=0, axis_index_group...  49.3 us
    all_to_all x1, starting transfers between devices, exchanged(): lax.all_to_all(value, axis, split_axis=0, concat_axis=0, axis_index_group...  17.1 us
    all_to_all x1, waiting for transfers between devices, exchanged(): lax.all_to_all(value, axis, split_axis=0, concat_axis=0, axis_index_group...  6.83 us
    pallas_call x1, Pallas kernels, local(): pl.pallas_call(basis_kernel, in_specs=[vmem, vmem], out_specs=(pl.BlockSp...  5.75 us
    unnamed x8, local copies, waits for them, and re-layouts  3.05 us
    pallas_call x1, Pallas kernels, local(): pl.pallas_call(step_kernel, out_shape=(jax.ShapeDtypeStruct((2, COLS, SHA...  2.89 us
    pallas_call x1, Pallas kernels, local(): pl.pallas_call(edges_kernel, in_specs=[hbm, hbm], out_specs=vmem, out_sha...  1.92 us
  transfers between devices with their start and end apart: 1, of which 1 were waited for; matrix products, arithmetic and copies ran while one was open for 0% of the time, Pallas kernels for 0%

profile of v4, /device:TPU:1, one launch (start us, length us, event | category | flops | bytes accessed | tf_op | source)
XLA Modules:
  0.0 88.5 jit_solution(10092941401586890068)
XLA Ops:
  0.6 1.9 %shard_map.69 = f32[64,1,128]{2,1,0:T(1,128)} custom-call(f32[256,128]{1,0:T(8,128)} %bitcast.8, f32[128,128]{1,0:T(8,128)} %bitcast.10), custom_call_target="tpu_custom_call" | custom-call | tf_op jit(solution)/shard_map/pallas_call | solution.py:363
  2.6 17.1 %all-to-all-start = ((f32[64,1,128]{2,1,0:T(1,128)}), f32[64,1,128]{2,1,0:T(1,128)S(1)}, u32[]{:S(2)}, u32[]{:S(2)}) async-start(f32[64,1,128]{2,1,0:T(1,128)} %shard_map.69), calls=%async_computation | async-start | bytes 65536 | tf_op jit(solution)/shard_map/all_to_all | solution.py:352
  20.4 0.0 copy-start
  20.4 0.9 %copy-done = f32[1,2,16384]{2,1,0:T(2,128)S(1)} copy-done((f32[1,2,16384]{2,1,0:T(2,128)S(1)}, f32[1,2,16384]{2,1,0:T(2,128)}, u32[]{:S(2)}) %copy-start) | copy-done | bytes 131096
  21.3 0.0 copy-start.1
  21.3 0.8 copy-done.1
  22.1 0.0 copy-start.2
  22.1 0.7 copy-done.2
  22.8 0.0 copy-start.3
  22.8 0.7 copy-done.3
  23.4 0.2 shard_map.68
  23.7 6.8 %all-to-all-done.edge_ref = f32[64,1,128]{2,1,0:T(1,128)S(1)} async-done(((f32[64,1,128]{2,1,0:T(1,128)}), f32[64,1,128]{2,1,0:T(1,128)S(1)}, u32[]{:S(2)}, u32[]{:S(2)}) %all-to-all-start) | async-done | bytes 32800 | tf_op jit(solution)/shard_map/all_to_all | solution.py:352
  30.5 0.1 shard_map.70
  30.6 11.7 %all_to_all.30 = f32[8,40,128]{2,1,0:T(8,128)S(1)} all-to-all(f32[8,40,128]{2,1,0:T(8,128)S(1)} %shard_map.70), channel_id=1, replica_groups=mesh['scen'=8,'reach'=64] {'scen'}, dimensions={0} | all-to-all | bytes 327680 | tf_op jit(solution)/shard_map/all_to_all | solution.py:352
  42.3 2.9 %shard_map.71 = (bf16[2,128,2048]{2,1,0:T(8,128)(2,1)S(1)}, f32[8,3,4,128]{3,2,1,0:T(4,128)S(1)}) custom-call(f32[320,128]{1,0:T(8,128)S(1)} %bitcast.7, f32[64,1,128]{2,1,0:T(1,128)S(1)} %all-to-all-done.edge_ref, f32[48,128]{1,0:T(8,128)S(1)} %get-tuple-element.7.aux_ref), custom_call_target="tpu_custom_call" | custom-call | tf_op jit(solution)/shard_map/pallas_call | solution.py:394
  45.2 8.1 %all_to_all.31.in_ref = f32[8,3,4,128]{3,2,1,0:T(4,128)S(1)} all-to-all(f32[8,3,4,128]{3,2,1,0:T(4,128)S(1)} %get-tuple-element.8), channel_id=1, replica_groups=mesh['scen'=8,'reach'=64] {'scen'}, dimensions={0} | all-to-all | bytes 98304 | tf_op jit(solution)/shard_map/all_to_all | solution.py:352
  53.3 9.5 %all_to_all.32.in_ref = f32[8,3,4,128]{3,2,1,0:T(4,128)S(1)} all-to-all(f32[8,3,4,128]{3,2,1,0:T(4,128)S(1)} %shard_map.72), channel_id=1, replica_groups={{0,1,2,3,4,5,6,7},{8,9,10,11,12,13,14,15},{16,17,18,19,20,21,22,23},{24..., dimensions={0} | all-to-all | bytes 98304 | tf_op jit(solution)/shard_map/all_to_all | solution.py:352
  62.8 9.4 %all_to_all.33.in_ref = f32[8,3,4,128]{3,2,1,0:T(4,128)S(1)} all-to-all(f32[8,3,4,128]{3,2,1,0:T(4,128)S(1)} %shard_map.73), channel_id=1, replica_groups={{0,8,16,24,32,40,48,56},{1,9,17,25,33,41,49,57},{2,10,18,26,34,42,50,58..., dimensions={0} | all-to-all | bytes 98304 | tf_op jit(solution)/shard_map/all_to_all | solution.py:352
  72.2 10.6 %all_to_all.34.gram_ref = f32[8,3,4,128]{3,2,1,0:T(4,128)S(1)} all-to-all(f32[8,3,4,128]{3,2,1,0:T(4,128)S(1)} %shard_map.74), channel_id=1, replica_groups=mesh['scen'=8,'reach'=64] {'scen'}, dimensions={0} | all-to-all | bytes 98304 | tf_op jit(solution)/shard_map/all_to_all | solution.py:352
  82.8 5.7 %shard_map.75 = (f32[2,2048,128]{2,1,0:T(8,128)}, f32[128,128]{1,0:T(8,128)}) custom-call(f32[8,3,4,128]{3,2,1,0:T(4,128)S(1)} %all_to_all.34.gram_ref, bf16[2,128,2048]{2,1,0:T(8,128)(2,1)S(1)} %get-tuple-element.9.cols_ref), custom_call_target="tpu_custom_call" | custom-call | tf_op jit(solution)/shard_map/pallas_call | solution.py:415
  (3 shorter events, 0.0 us)
Async XLA Ops:
  2.6 27.9 %all-to-all-start = ((f32[64,1,128]{2,1,0:T(1,128)}), f32[64,1,128]{2,1,0:T(1,128)S(1)}, u32[]{:S(2)}, u32[]{:S(2)}) async-start(f32[64,1,128]{2,1,0:T(1,128)} %shard_map.69), calls=%async_computation | async-start | bytes 65536 | tf_op jit(solution)/shard_map/all_to_all | solution.py:352
  20.4 0.9 %copy-start = (f32[1,2,16384]{2,1,0:T(2,128)S(1)}, f32[1,2,16384]{2,1,0:T(2,128)}, u32[]{:S(2)}) copy-start(f32[1,2,16384]{2,1,0:T(2,128)} %param.5) | copy-start | bytes 393220
  21.3 0.8 copy-start.1
  22.1 0.7 copy-start.2
  22.8 0.7 copy-start.3

commit v5 on v4

--- a/solution.py
+++ b/solution.py
@@ -20,9 +20,7 @@
 BLOCKS = SHARE // LANES
 RIGHT_ROW = 2 * BLOCKS
 LEFT_ROW = RIGHT_ROW + 2
-HEAD_ROW = LEFT_ROW + 2
-VALVE_ROW = HEAD_ROW + 1
-FLOW_ROW = VALVE_ROW + 1
+PLAN_ROW = LEFT_ROW + 2
 WINDOW = 40
 WIDE = BLOCKS + 2
 PANEL = 64
@@ -79,7 +77,7 @@
     return jnp.where(lane < HALO, moved, 0.0)
 
 
-def window_kernel(state_ref, resist_ref, flow_ref, head_ref, valve_ref, out_ref, aux_ref):
+def window_kernel(state_ref, resist_ref, plan_ref, out_ref, aux_ref):
     rows = 2 * BLOCKS
     none = jnp.zeros((2, LANES), jnp.float32)
     for which in range(SCENS):
@@ -88,10 +86,8 @@
         after = state_ref[start + rows : start + rows + 2, :] if which < SCENS - 1 else none
         out_ref[which, RIGHT_ROW : RIGHT_ROW + 2, :] = after
         out_ref[which, LEFT_ROW : LEFT_ROW + 2, :] = state_ref[start - 2 : start, :] if which > 0 else none
-        out_ref[which, HEAD_ROW:WINDOW, :] = jnp.zeros((WINDOW - HEAD_ROW, LANES), jnp.float32)
-        out_ref[which, HEAD_ROW : HEAD_ROW + 1, 0:STEPS] = head_ref[...]
-        out_ref[which, VALVE_ROW : VALVE_ROW + 1, 0:STEPS] = valve_ref[...]
-        out_ref[which, FLOW_ROW : FLOW_ROW + 1, :] = jnp.full((1, LANES), flow_ref[0], jnp.float32)
+        out_ref[which, PLAN_ROW:WINDOW, :] = jnp.zeros((WINDOW - PLAN_ROW, LANES), jnp.float32)
+        out_ref[which, PLAN_ROW : PLAN_ROW + 1, 0 : 2 * STEPS + 1] = plan_ref[...]
 
     scen = lax.axis_index("scen")
     first = scen * BLOCKS
@@ -142,8 +138,8 @@
     def taken(row):
         return win_ref[pl.ds(row, SCENS, stride=WINDOW), :]
 
-    head_plan = taken(HEAD_ROW)
-    valve_plan = taken(VALVE_ROW)
+    plans = taken(PLAN_ROW)
+    head_plan, valve_plan = plans[:, 0:STEPS], plans[:, STEPS : 2 * STEPS]
     orifice = 1.0 / (1.0 + valve_plan)
     opened = valve_plan * orifice
     for moment in range(STEPS):
@@ -151,7 +147,7 @@
             plan_ref[which, moment * SCENS : (moment + 1) * SCENS, :] = jnp.broadcast_to(
                 plan[:, moment : moment + 1], (SCENS, LANES)
             )
-    steady = taken(FLOW_ROW)
+    steady = jnp.broadcast_to(plans[:, 2 * STEPS : 2 * STEPS + 1], (SCENS, LANES))
     scale = steady * jnp.abs(steady) * (1.0 / CELLS)
     mean_flow = steady * CELLS ** (-0.5)
     first_head = plan_ref[0, 0:SCENS, :]
@@ -355,7 +351,6 @@
 def local(perturb, resist, flow_rate, head_plan, valve_plan):
     f32 = jnp.float32
     vmem = pl.BlockSpec(memory_space=pltpu.VMEM)
-    smem = pl.BlockSpec(memory_space=pltpu.SMEM)
     hbm = pl.BlockSpec(memory_space=pltpu.HBM)
     blocks = PART // LANES
     state = perturb.reshape(2, blocks, LANES).transpose(1, 0, 2).reshape(2 * blocks, LANES)
@@ -373,15 +368,16 @@
         compiler_params=params(61),
     )(state, resist)
     edges = exchanged(edges, "reach")
+    plans = jnp.concatenate([head_plan, valve_plan, flow_rate.reshape(1, 1)], axis=1)
     windows, aux = pl.pallas_call(
         window_kernel,
-        in_specs=[vmem, vmem, smem, vmem, vmem],
+        in_specs=[vmem, vmem, vmem],
         out_shape=(
             jax.ShapeDtypeStruct((SCENS, WINDOW, LANES), f32),
             jax.ShapeDtypeStruct((48, LANES), f32),
         ),
         compiler_params=params(),
-    )(state, resist, flow_rate, head_plan, valve_plan)
+    )(state, resist, plans)
     windows = pl.pallas_call(
         patch_kernel,
         in_specs=[vmem, vmem],

time: 89 us -> 88.6 us (level)
  local copies, waits for them, and re-layouts: 3.05 us -> 1.74 us
    unnamed x8 -> x4, local copies, waits for them, and re-layouts: 3.05 us -> 1.74 us
  transfers between devices with their start and end apart: 1 -> 1, of which waited for: 1 -> 1; matrix products, arithmetic and copies ran while one was open for 0% -> 1% of each run, Pallas kernels for 0% -> 0%
where the time goes in v5:
time: 88.6 us; the launch traced here: 88.1 us
  blocking collectives  48.9 us (55%)
  starting transfers between devices  17.1 us (19%)
  Pallas kernels  10.9 us (12%)
  waiting for transfers between devices  7.39 us (8%)
  local copies, waits for them, and re-layouts  1.74 us (2%)
  between operations  1.31 us (1%)
    all_to_all x5, blocking collectives, exchanged(): lax.all_to_all(value, axis, split_axis=0, concat_axis=0, axis_index_group...  48.9 us
    all_to_all x1, starting transfers between devices, exchanged(): lax.all_to_all(value, axis, split_axis=0, concat_axis=0, axis_index_group...  17.1 us
    all_to_all x1, waiting for transfers between devices, exchanged(): lax.all_to_all(value, axis, split_axis=0, concat_axis=0, axis_index_group...  7.39 us
    pallas_call x1, Pallas kernels, local(): pl.pallas_call(basis_kernel, in_specs=[vmem, vmem], out_specs=(pl.BlockSp...  5.75 us
    pallas_call x1, Pallas kernels, local(): pl.pallas_call(step_kernel, out_shape=(jax.ShapeDtypeStruct((2, COLS, SHA...  2.9 us
    pallas_call x1, Pallas kernels, local(): pl.pallas_call(edges_kernel, in_specs=[hbm, hbm], out_specs=vmem, out_sha...  1.92 us
  transfers between devices with their start and end apart: 1, of which 1 were waited for; matrix products, arithmetic and copies ran while one was open for 1% of the time, Pallas kernels for 0%

profile of v5, /device:TPU:1, one launch (start us, length us, event | category | flops | bytes accessed | tf_op | source)
XLA Modules:
  0.0 88.1 jit_solution(15990919216601957092)
XLA Ops:
  0.6 1.9 %shard_map.69 = f32[64,1,128]{2,1,0:T(1,128)} custom-call(f32[256,128]{1,0:T(8,128)} %bitcast.10, f32[128,128]{1,0:T(8,128)} %bitcast.12), custom_call_target="tpu_custom_call" | custom-call | tf_op jit(solution)/shard_map/pallas_call | solution.py:358
  2.6 17.1 %all-to-all-start = ((f32[64,1,128]{2,1,0:T(1,128)}), f32[64,1,128]{2,1,0:T(1,128)S(1)}, u32[]{:S(2)}, u32[]{:S(2)}) async-start(f32[64,1,128]{2,1,0:T(1,128)} %shard_map.69), calls=%async_computation | async-start | bytes 65536 | tf_op jit(solution)/shard_map/all_to_all | solution.py:348
  20.4 0.7 pad_maximum_fusion.plan_ref
  21.1 0.0 copy-start
  21.1 0.9 %copy-done = f32[1,2,16384]{2,1,0:T(2,128)S(1)} copy-done((f32[1,2,16384]{2,1,0:T(2,128)S(1)}, f32[1,2,16384]{2,1,0:T(2,128)}, u32[]{:S(2)}) %copy-start) | copy-done | bytes 131096
  22.0 0.0 copy-start.1
  22.0 0.8 copy-done.1
  22.9 0.2 shard_map.68
  23.1 7.4 %all-to-all-done.edge_ref = f32[64,1,128]{2,1,0:T(1,128)S(1)} async-done(((f32[64,1,128]{2,1,0:T(1,128)}), f32[64,1,128]{2,1,0:T(1,128)S(1)}, u32[]{:S(2)}, u32[]{:S(2)}) %all-to-all-start) | async-done | bytes 32800 | tf_op jit(solution)/shard_map/all_to_all | solution.py:348
  30.5 0.1 shard_map.70
  30.6 11.7 %all_to_all.30 = f32[8,40,128]{2,1,0:T(8,128)S(1)} all-to-all(f32[8,40,128]{2,1,0:T(8,128)S(1)} %shard_map.70), channel_id=1, replica_groups=mesh['scen'=8,'reach'=64] {'scen'}, dimensions={0} | all-to-all | bytes 327680 | tf_op jit(solution)/shard_map/all_to_all | solution.py:348
  42.3 2.9 %shard_map.71 = (bf16[2,128,2048]{2,1,0:T(8,128)(2,1)S(1)}, f32[8,3,4,128]{3,2,1,0:T(4,128)S(1)}) custom-call(f32[320,128]{1,0:T(8,128)S(1)} %bitcast.9, f32[64,1,128]{2,1,0:T(1,128)S(1)} %all-to-all-done.edge_ref, f32[48,128]{1,0:T(8,128)S(1)} %get-tuple-element.7.aux_ref), custom_call_target="tpu_custom_call" | custom-call | tf_op jit(solution)/shard_map/pallas_call | solution.py:390
  45.2 8.1 %all_to_all.31.in_ref = f32[8,3,4,128]{3,2,1,0:T(4,128)S(1)} all-to-all(f32[8,3,4,128]{3,2,1,0:T(4,128)S(1)} %get-tuple-element.8), channel_id=1, replica_groups=mesh['scen'=8,'reach'=64] {'scen'}, dimensions={0} | all-to-all | bytes 98304 | tf_op jit(solution)/shard_map/all_to_all | solution.py:348
  53.3 9.5 %all_to_all.32.in_ref = f32[8,3,4,128]{3,2,1,0:T(4,128)S(1)} all-to-all(f32[8,3,4,128]{3,2,1,0:T(4,128)S(1)} %shard_map.72), channel_id=1, replica_groups={{0,1,2,3,4,5,6,7},{8,9,10,11,12,13,14,15},{16,17,18,19,20,21,22,23},{24..., dimensions={0} | all-to-all | bytes 98304 | tf_op jit(solution)/shard_map/all_to_all | solution.py:348
  62.8 9.4 %all_to_all.33.in_ref = f32[8,3,4,128]{3,2,1,0:T(4,128)S(1)} all-to-all(f32[8,3,4,128]{3,2,1,0:T(4,128)S(1)} %shard_map.73), channel_id=1, replica_groups={{0,8,16,24,32,40,48,56},{1,9,17,25,33,41,49,57},{2,10,18,26,34,42,50,58..., dimensions={0} | all-to-all | bytes 98304 | tf_op jit(solution)/shard_map/all_to_all | solution.py:348
  72.2 10.1 %all_to_all.34.gram_ref = f32[8,3,4,128]{3,2,1,0:T(4,128)S(1)} all-to-all(f32[8,3,4,128]{3,2,1,0:T(4,128)S(1)} %shard_map.74), channel_id=1, replica_groups=mesh['scen'=8,'reach'=64] {'scen'}, dimensions={0} | all-to-all | bytes 98304 | tf_op jit(solution)/shard_map/all_to_all | solution.py:348
  82.4 5.7 %shard_map.75 = (f32[2,2048,128]{2,1,0:T(8,128)}, f32[128,128]{1,0:T(8,128)}) custom-call(f32[8,3,4,128]{3,2,1,0:T(4,128)S(1)} %all_to_all.34.gram_ref, bf16[2,128,2048]{2,1,0:T(8,128)(2,1)S(1)} %get-tuple-element.9.cols_ref), custom_call_target="tpu_custom_call" | custom-call | tf_op jit(solution)/shard_map/pallas_call | solution.py:411
  (3 shorter events, 0.0 us)
Async XLA Ops:
  2.6 27.9 %all-to-all-start = ((f32[64,1,128]{2,1,0:T(1,128)}), f32[64,1,128]{2,1,0:T(1,128)S(1)}, u32[]{:S(2)}, u32[]{:S(2)}) async-start(f32[64,1,128]{2,1,0:T(1,128)} %shard_map.69), calls=%async_computation | async-start | bytes 65536 | tf_op jit(solution)/shard_map/all_to_all | solution.py:348
  21.1 0.9 %copy-start = (f32[1,2,16384]{2,1,0:T(2,128)S(1)}, f32[1,2,16384]{2,1,0:T(2,128)}, u32[]{:S(2)}) copy-start(f32[1,2,16384]{2,1,0:T(2,128)} %param.5) | copy-start | bytes 393220
  22.0 0.8 copy-start.1

commit v6 on v5

--- a/solution.py
+++ b/solution.py
@@ -22,7 +22,7 @@
 LEFT_ROW = RIGHT_ROW + 2
 PLAN_ROW = LEFT_ROW + 2
 WINDOW = 40
-WIDE = BLOCKS + 2
+WIDE = BLOCKS + 1
 PANEL = 64
 CHUNK = 256
 HALF = COLS // 2
@@ -49,19 +49,29 @@
     lane = lax.broadcasted_iota(jnp.int32, (1, LANES), 1)
     is_first, is_final = lane < HALO, lane >= LANES - HALO
     total = jnp.sum(jnp.sum(resist[...], axis=0, keepdims=True), axis=1, keepdims=True)
-    outer = jnp.where(is_first, resist[0:1, :], jnp.where(is_final, resist[LANES - 1 : LANES, :], 0.0))
-    upto = outer
-    for step in (1, 2, 4, 8):
-        upto = upto + jnp.where(lane >= step, pltpu.roll(upto, step, 1), 0.0)
-    back = jnp.where(lane == LANES - 1, total, upto - upto[:, LANES - 1 : LANES])
-    firsts = (ends[0, 0:1, :], ends[0, 1:2, :], resist[0:1, :], upto)
-    finals = (ends[1, 6:7, :], ends[1, 7:8, :], resist[LANES - 1 : LANES, :], back)
-    row = jnp.zeros((1, LANES), jnp.float32)
-    for place, (first, final) in enumerate(zip(firsts, finals)):
-        low, high = jnp.where(is_first, first, 0.0), jnp.where(is_final, final, 0.0)
-        if place:
-            low, high = pltpu.roll(low, place * HALO, 1), pltpu.roll(high, LANES - place * HALO, 1)
-        row = row + low + high
+    firsts = [jnp.where(is_first, row, 0.0) for row in (ends[0, 0:1, :], ends[0, 1:2, :], resist[0:1, :])]
+    finals = [
+        jnp.where(is_final, row, 0.0) for row in (ends[1, 6:7, :], ends[1, 7:8, :], resist[LANES - 1 : LANES, :])
+    ]
+
+    def moved(row, by):
+        return pltpu.roll(row, by % LANES, 1) if by % LANES else row
+
+    row = firsts[0] + finals[0]
+    for place in (1, 2):
+        row = row + moved(firsts[place], place * HALO) + moved(finals[place], -place * HALO)
+    ahead, behind = firsts[2], moved(finals[2], -1)
+    for step in (1, 2, 3):
+        ahead = ahead + moved(firsts[2], step)
+        behind = behind + moved(finals[2], -1 - step)
+    at = 3 * HALO
+    upto, rest = moved(ahead, at), moved(behind, -at)
+    for step in (4, 8, 12):
+        upto = upto + moved(ahead, at + step)
+        rest = rest + moved(behind, -at - step)
+    row = jnp.where((lane >= at) & (lane < at + HALO), upto, row)
+    row = jnp.where((lane >= LANES - at - HALO) & (lane < LANES - at), -rest, row)
+    row = jnp.where(lane == LANES - at - 1, total, row)
     out_ref[...] = jnp.broadcast_to(row[None], (REACHES, 1, LANES))
 
 
@@ -159,22 +169,25 @@
     previous = edge_ref[jnp.maximum(reach - 1, 0)]
     following = edge_ref[jnp.minimum(reach + 1, REACHES - 1)]
     none = jnp.zeros((SCENS, LANES), jnp.float32)
+    is_left = lane >= LANES // 2
+
+    def outer(row, at, beyond, base, edge, upto):
+        resist = jnp.where(beyond, edge, aux_ref[at : at + 1, :])
+        running = jnp.where(beyond, base + upto, upstream + aux_ref[24 + at : 25 + at, :])
+        return taken(row), taken(row + 1), resist, running
+
+    before = jnp.where(is_high[0:1], 0.0, last_of(previous, 3))
+    left = outer(LEFT_ROW, BLOCKS + 1, scen == 0, upstream, last_of(previous, 2), before)
+    right = outer(
+        RIGHT_ROW, BLOCKS, scen == SCENS - 1, through, first_of(following, 2), first_of(following, 3)
+    )
     for j in range(WIDE):
-        row = [LEFT_ROW, RIGHT_ROW][j > BLOCKS] if j in (0, WIDE - 1) else 2 * (j - 1)
-        at = [BLOCKS + 1, BLOCKS][j > BLOCKS] if j in (0, WIDE - 1) else j - 1
-        resist = aux_ref[at : at + 1, :]
-        running = upstream + aux_ref[24 + at : 25 + at, :]
-        head, flow = taken(row), taken(row + 1)
-        if j in (0, WIDE - 1):
-            if j == 0:
-                beyond, base = scen == 0, upstream
-                edge, upto = last_of(previous, 2), last_of(previous, 3)
-                upto = jnp.where(is_high[0:1], 0.0, upto)
-            else:
-                beyond, base = scen == SCENS - 1, through
-                edge, upto = first_of(following, 2), first_of(following, 3)
-            resist = jnp.where(beyond, edge, resist)
-            running = jnp.where(beyond, base + upto, running)
+        if j == 0:
+            head, flow, resist, running = (jnp.where(is_left, a, b) for a, b in zip(left, right))
+        else:
+            head, flow = taken(2 * (j - 1)), taken(2 * (j - 1) + 1)
+            resist = aux_ref[j - 1 : j, :]
+            running = upstream + aux_ref[23 + j : 24 + j, :]
         wide_ref[0, j] = first_head - running * scale + head
         wide_ref[1, j] = mean_flow + flow
         for state in range(4):
@@ -196,11 +209,10 @@
                 net = flow - friction
                 return pltpu.roll(head + net, 1, 1), pltpu.roll(head - net, LANES - 1, 1)
 
-            forward_before, (forward, backward) = None, sent(0)
+            ring_start, ring_end = sent(0), sent(WIDE - 1)
+            forward_before, (forward, backward) = ring_end[0], ring_start
             for j in range(WIDE):
-                forward_after, backward_after = sent(j + 1) if j + 1 < WIDE else (forward, backward)
-                if forward_before is None:
-                    forward_before = forward
+                forward_after, backward_after = {WIDE - 2: ring_end, WIDE - 1: ring_start}.get(j) or sent(j + 1)
                 from_left = jnp.where(is_low, forward_before, forward)
                 from_right = jnp.where(is_high, backward_after, backward)
                 new_head = 0.5 * (from_left + from_right)
@@ -401,11 +413,8 @@
         ],
         compiler_params=params(),
     )(windows, edges, aux)
-    along = [[RING * a + b for b in range(RING)] for a in range(RING)]
-    across = [[RING * b + a for b in range(RING)] for a in range(RING)]
-    gram = fold(exchanged(gram, "scen"), RING)
-    gram = fold(exchanged(gram, "reach", along), RING)
-    gram = fold(exchanged(gram, "reach", across), SCENS)
+    gram = fold(exchanged(gram, "scen"), REACHES)
+    gram = fold(exchanged(gram, "reach"), SCENS)
     gram = exchanged(gram, "scen")
     chunks = 2 * SHARE // CHUNK
     return pl.pallas_call(

time: 88.6 us -> 88.1 us (level)
    all_to_all x5 -> x4, blocking collectives: 48.9 us -> 48.6 us  [exchanged(): lax.all_to_all(value, axis, split_axis=0, concat_axis=0, axis_index_group...]
where the time goes in v6:
time: 88.1 us; the launch traced here: 87.6 us
  blocking collectives  48.6 us (55%)
  starting transfers between devices  17.1 us (19%)
  Pallas kernels  10.7 us (12%)
  waiting for transfers between devices  7.39 us (8%)
  local copies, waits for them, and re-layouts  1.74 us (2%)
  between operations  1.31 us (1%)
    all_to_all x4, blocking collectives, exchanged(): lax.all_to_all(value, axis, split_axis=0, concat_axis=0, axis_index_group...  48.6 us
    all_to_all x1, starting transfers between devices, exchanged(): lax.all_to_all(value, axis, split_axis=0, concat_axis=0, axis_index_group...  17.1 us
    all_to_all x1, waiting for transfers between devices, exchanged(): lax.all_to_all(value, axis, split_axis=0, concat_axis=0, axis_index_group...  7.39 us
    pallas_call x1, Pallas kernels, local(): pl.pallas_call(basis_kernel, in_specs=[vmem, vmem], out_specs=(pl.BlockSp...  5.75 us
    pallas_call x1, Pallas kernels, local(): pl.pallas_call(step_kernel, out_shape=(jax.ShapeDtypeStruct((2, COLS, SHA...  2.83 us
  transfers between devices with their start and end apart: 1, of which 1 were waited for; matrix products, arithmetic and copies ran while one was open for 1% of the time, Pallas kernels for 0%

profile of v6, /device:TPU:1, one launch (start us, length us, event | category | flops | bytes accessed | tf_op | source)
XLA Modules:
  0.0 87.6 jit_solution(13781032633139833918)
XLA Ops:
  0.6 1.7 %shard_map.69 = f32[64,1,128]{2,1,0:T(1,128)} custom-call(f32[256,128]{1,0:T(8,128)} %bitcast.10, f32[128,128]{1,0:T(8,128)} %bitcast.12), custom_call_target="tpu_custom_call" | custom-call | tf_op jit(solution)/shard_map/pallas_call | solution.py:370
  2.3 17.1 %all-to-all-start = ((f32[64,1,128]{2,1,0:T(1,128)}), f32[64,1,128]{2,1,0:T(1,128)S(1)}, u32[]{:S(2)}, u32[]{:S(2)}) async-start(f32[64,1,128]{2,1,0:T(1,128)} %shard_map.69), calls=%async_computation | async-start | bytes 65536 | tf_op jit(solution)/shard_map/all_to_all | solution.py:360
  20.1 0.7 pad_maximum_fusion.plan_ref
  20.9 0.0 copy-start
  20.9 0.9 %copy-done = f32[1,2,16384]{2,1,0:T(2,128)S(1)} copy-done((f32[1,2,16384]{2,1,0:T(2,128)S(1)}, f32[1,2,16384]{2,1,0:T(2,128)}, u32[]{:S(2)}) %copy-start) | copy-done | bytes 131096
  21.8 0.0 copy-start.1
  21.8 0.8 copy-done.1
  22.6 0.2 shard_map.68
  22.8 7.4 %all-to-all-done.edge_ref = f32[64,1,128]{2,1,0:T(1,128)S(1)} async-done(((f32[64,1,128]{2,1,0:T(1,128)}), f32[64,1,128]{2,1,0:T(1,128)S(1)}, u32[]{:S(2)}, u32[]{:S(2)}) %all-to-all-start) | async-done | bytes 32800 | tf_op jit(solution)/shard_map/all_to_all | solution.py:360
  30.2 0.1 shard_map.70
  30.3 11.7 %all_to_all.25 = f32[8,40,128]{2,1,0:T(8,128)S(1)} all-to-all(f32[8,40,128]{2,1,0:T(8,128)S(1)} %shard_map.70), channel_id=1, replica_groups=mesh['scen'=8,'reach'=64] {'scen'}, dimensions={0} | all-to-all | bytes 327680 | tf_op jit(solution)/shard_map/all_to_all | solution.py:360
  42.1 2.8 %shard_map.71 = (bf16[2,128,2048]{2,1,0:T(8,128)(2,1)S(1)}, f32[8,3,4,128]{3,2,1,0:T(4,128)S(1)}) custom-call(f32[320,128]{1,0:T(8,128)S(1)} %bitcast.9, f32[64,1,128]{2,1,0:T(1,128)S(1)} %all-to-all-done.edge_ref, f32[48,128]{1,0:T(8,128)S(1)} %get-tuple-element.7.aux_ref), custom_call_target="tpu_custom_call" | custom-call | tf_op jit(solution)/shard_map/pallas_call | solution.py:402
  44.9 8.1 %all_to_all.26.in_ref = f32[8,3,4,128]{3,2,1,0:T(4,128)S(1)} all-to-all(f32[8,3,4,128]{3,2,1,0:T(4,128)S(1)} %get-tuple-element.8), channel_id=1, replica_groups=mesh['scen'=8,'reach'=64] {'scen'}, dimensions={0} | all-to-all | bytes 98304 | tf_op jit(solution)/shard_map/all_to_all | solution.py:360
  53.0 0.1 shard_map.72
  53.0 18.6 %all_to_all.27.in_ref = f32[64,3,4,128]{3,2,1,0:T(4,128)S(1)} all-to-all(f32[64,3,4,128]{3,2,1,0:T(4,128)S(1)} %shard_map.72), channel_id=1, replica_groups=mesh['scen'=8,'reach'=64] {'reach'}, dimensions={0} | all-to-all | bytes 786432 | tf_op jit(solution)/shard_map/all_to_all | solution.py:360
  71.6 0.1 shard_map.73
  71.7 10.2 %all_to_all.28.gram_ref = f32[8,3,4,128]{3,2,1,0:T(4,128)S(1)} all-to-all(f32[8,3,4,128]{3,2,1,0:T(4,128)S(1)} %shard_map.73), channel_id=1, replica_groups=mesh['scen'=8,'reach'=64] {'scen'}, dimensions={0} | all-to-all | bytes 98304 | tf_op jit(solution)/shard_map/all_to_all | solution.py:360
  81.9 5.7 %shard_map.74 = (f32[2,2048,128]{2,1,0:T(8,128)}, f32[128,128]{1,0:T(8,128)}) custom-call(f32[8,3,4,128]{3,2,1,0:T(4,128)S(1)} %all_to_all.28.gram_ref, bf16[2,128,2048]{2,1,0:T(8,128)(2,1)S(1)} %get-tuple-element.9.cols_ref), custom_call_target="tpu_custom_call" | custom-call | tf_op jit(solution)/shard_map/pallas_call | solution.py:420
Async XLA Ops:
  2.3 27.9 %all-to-all-start = ((f32[64,1,128]{2,1,0:T(1,128)}), f32[64,1,128]{2,1,0:T(1,128)S(1)}, u32[]{:S(2)}, u32[]{:S(2)}) async-start(f32[64,1,128]{2,1,0:T(1,128)} %shard_map.69), calls=%async_computation | async-start | bytes 65536 | tf_op jit(solution)/shard_map/all_to_all | solution.py:360
  20.9 0.9 %copy-start = (f32[1,2,16384]{2,1,0:T(2,128)S(1)}, f32[1,2,16384]{2,1,0:T(2,128)}, u32[]{:S(2)}) copy-start(f32[1,2,16384]{2,1,0:T(2,128)} %param.5) | copy-start | bytes 393220
  21.8 0.8 copy-start.1

commit v7 on v6

--- a/solution.py
+++ b/solution.py
@@ -27,7 +27,7 @@
 CHUNK = 256
 HALF = COLS // 2
 QUARTER = COLS // 4
-PIECES = 3
+PIECES = 5
 EXACT = lax.Precision.HIGHEST
 
 
@@ -253,13 +253,18 @@
     rows = [order_ref[pl.ds(which, STEPS, stride=SCENS), :] for which in range(SCENS)]
     order_ref[...] = jnp.concatenate(rows, axis=0).T
     rows = [order_ref[pl.ds(which, STEPS, stride=SCENS), :] for which in range(SCENS)]
-    high = lax.broadcasted_iota(jnp.int32, (QUARTER, COLS), 1) >= HALF
-    upper, lower = jnp.concatenate(rows[4:6], axis=0), jnp.concatenate(rows[6:8], axis=0)
-    packed = jnp.concatenate(rows[0:4] + [jnp.where(high, upper, pltpu.roll(lower, HALF, 1))], axis=0)
+    quarters = [jnp.concatenate(rows[2 * which : 2 * which + 2], axis=0) for which in range(4)]
+    column = lax.broadcasted_iota(jnp.int32, (QUARTER, COLS), 1) // QUARTER
+    second = jnp.where(column == 0, pltpu.roll(quarters[2], 2 * QUARTER, 1), quarters[1])
+    rest, column = pltpu.roll(rows[7], QUARTER, 1), column[0:STEPS]
+    for place, piece in ((1, rows[6]), (2, rows[5]), (3, rows[4])):
+        moved = pltpu.roll(piece, (place + 1) * QUARTER, 1) if place < 3 else piece
+        rest = jnp.where(column == place, moved, rest)
+    packed = jnp.concatenate([quarters[0], second, rest], axis=0)
     for which in range(SCENS):
         for part in range(PIECES):
-            at = (which * PIECES + part) * 4
-            gram_ref[which, part] = packed[at : at + 4, :]
+            at = (which * PIECES + part) * 2
+            gram_ref[which, part] = packed[at : at + 2, :]
 
 
 def fold_kernel(in_ref, out_ref):
@@ -281,9 +286,19 @@
             turned_ref[field * (SHARE // CHUNK) + part] = cols_ref[field, :, part * CHUNK : (part + 1) * CHUNK].T
     for which in range(SCENS):
         for part in range(PIECES):
-            at = (which * PIECES + part) * 4
-            work_ref[at : at + 4, 0:COLS] = gram_ref[which, part] * scale
-    work_ref[HALF + QUARTER :, 0:COLS] = pltpu.roll(work_ref[HALF : HALF + QUARTER, 0:COLS], HALF, 1)
+            at = (which * PIECES + part) * 2
+            order_ref[at : at + 2, :] = gram_ref[which, part] * scale
+    column = lax.broadcasted_iota(jnp.int32, (QUARTER, COLS), 1) // QUARTER
+    first, second = order_ref[0:QUARTER, :], order_ref[QUARTER:HALF, :]
+    rest = order_ref[HALF : HALF + STEPS, :]
+    third = jnp.concatenate([rest, pltpu.roll(rest, QUARTER, 1)], axis=0)
+    third = jnp.where(column == 3, third, pltpu.roll(second, 2 * QUARTER, 1))
+    fourth = jnp.concatenate([pltpu.roll(rest, 2 * QUARTER, 1), pltpu.roll(rest, 3 * QUARTER, 1)], axis=0)
+    mirror = jnp.concatenate([first, second, third, fourth], axis=0).T
+    work_ref[0:QUARTER, 0:COLS] = first
+    work_ref[QUARTER:HALF, 0:COLS] = jnp.where(column == 0, mirror[QUARTER:HALF, :], second)
+    work_ref[HALF : HALF + QUARTER, 0:COLS] = third
+    work_ref[HALF + QUARTER :, 0:COLS] = jnp.where(column == 2, mirror[HALF + QUARTER :, :], fourth)
     for g in range(COLS // 8):
         work_ref[8 * g : 8 * g + 8, COLS:] = jnp.where(lane == sub + 8 * g, 1.0, 0.0).astype(jnp.float32)
     inverse_rows = []
@@ -403,7 +418,7 @@
         step_kernel,
         out_shape=(
             jax.ShapeDtypeStruct((2, COLS, SHARE), jnp.bfloat16),
-            jax.ShapeDtypeStruct((SCENS, PIECES, 4, COLS), f32),
+            jax.ShapeDtypeStruct((SCENS, PIECES, 2, COLS), f32),
         ),
         scratch_shapes=[
             pltpu.VMEM((7, WIDE, SCENS, LANES), f32),

time: 88.1 us -> 87.2 us (0.990)
  blocking collectives: 48.6 us -> 47.6 us
    all_to_all x4, blocking collectives: 48.6 us -> 47.6 us  [exchanged(): lax.all_to_all(value, axis, split_axis=0, concat_axis=0, axis_index_group...]
where the time goes in v7:
time: 87.2 us; the launch traced here: 86.8 us
  blocking collectives  47.6 us (55%)
  starting transfers between devices  17.1 us (20%)
  Pallas kernels  10.8 us (12%)
  waiting for transfers between devices  7.39 us (8%)
  local copies, waits for them, and re-layouts  1.74 us (2%)
  between operations  1.32 us (2%)
    all_to_all x4, blocking collectives, exchanged(): lax.all_to_all(value, axis, split_axis=0, concat_axis=0, axis_index_group...  47.6 us
    all_to_all x1, starting transfers between devices, exchanged(): lax.all_to_all(value, axis, split_axis=0, concat_axis=0, axis_index_group...  17.1 us
    all_to_all x1, waiting for transfers between devices, exchanged(): lax.all_to_all(value, axis, split_axis=0, concat_axis=0, axis_index_group...  7.39 us
    pallas_call x1, Pallas kernels, local(): pl.pallas_call(basis_kernel, in_specs=[vmem, vmem], out_specs=(pl.BlockSp...  5.82 us
    pallas_call x1, Pallas kernels, local(): pl.pallas_call(step_kernel, out_shape=(jax.ShapeDtypeStruct((2, COLS, SHA...  2.84 us
    unnamed x4, local copies, waits for them, and re-layouts  1.74 us
  transfers between devices with their start and end apart: 1, of which 1 were waited for; matrix products, arithmetic and copies ran while one was open for 1% of the time, Pallas kernels for 0%

profile of v7, /device:TPU:1, one launch (start us, length us, event | category | flops | bytes accessed | tf_op | source)
XLA Modules:
  0.0 86.8 jit_solution(6549128520758193491)
XLA Ops:
  0.6 1.7 %shard_map.69 = f32[64,1,128]{2,1,0:T(1,128)} custom-call(f32[256,128]{1,0:T(8,128)} %bitcast.10, f32[128,128]{1,0:T(8,128)} %bitcast.12), custom_call_target="tpu_custom_call" | custom-call | tf_op jit(solution)/shard_map/pallas_call | solution.py:385
  2.3 17.1 %all-to-all-start = ((f32[64,1,128]{2,1,0:T(1,128)}), f32[64,1,128]{2,1,0:T(1,128)S(1)}, u32[]{:S(2)}, u32[]{:S(2)}) async-start(f32[64,1,128]{2,1,0:T(1,128)} %shard_map.69), calls=%async_computation | async-start | bytes 65536 | tf_op jit(solution)/shard_map/all_to_all | solution.py:375
  20.1 0.7 pad_maximum_fusion.plan_ref
  20.9 0.0 copy-start
  20.9 0.9 %copy-done = f32[1,2,16384]{2,1,0:T(2,128)S(1)} copy-done((f32[1,2,16384]{2,1,0:T(2,128)S(1)}, f32[1,2,16384]{2,1,0:T(2,128)}, u32[]{:S(2)}) %copy-start) | copy-done | bytes 131096
  21.8 0.0 copy-start.1
  21.8 0.8 copy-done.1
  22.6 0.2 shard_map.68
  22.8 7.4 %all-to-all-done.edge_ref = f32[64,1,128]{2,1,0:T(1,128)S(1)} async-done(((f32[64,1,128]{2,1,0:T(1,128)}), f32[64,1,128]{2,1,0:T(1,128)S(1)}, u32[]{:S(2)}, u32[]{:S(2)}) %all-to-all-start) | async-done | bytes 32800 | tf_op jit(solution)/shard_map/all_to_all | solution.py:375
  30.2 0.1 shard_map.70
  30.3 11.7 %all_to_all.25 = f32[8,40,128]{2,1,0:T(8,128)S(1)} all-to-all(f32[8,40,128]{2,1,0:T(8,128)S(1)} %shard_map.70), channel_id=1, replica_groups=mesh['scen'=8,'reach'=64] {'scen'}, dimensions={0} | all-to-all | bytes 327680 | tf_op jit(solution)/shard_map/all_to_all | solution.py:375
  42.1 2.8 %shard_map.71 = (bf16[2,128,2048]{2,1,0:T(8,128)(2,1)S(1)}, f32[8,5,2,128]{3,2,1,0:T(2,128)S(1)}) custom-call(f32[320,128]{1,0:T(8,128)S(1)} %bitcast.9, f32[64,1,128]{2,1,0:T(1,128)S(1)} %all-to-all-done.edge_ref, f32[48,128]{1,0:T(8,128)S(1)} %get-tuple-element.7.aux_ref), custom_call_target="tpu_custom_call" | custom-call | tf_op jit(solution)/shard_map/pallas_call | solution.py:417
  44.9 8.0 %all_to_all.26.in_ref = f32[8,5,2,128]{3,2,1,0:T(2,128)S(1)} all-to-all(f32[8,5,2,128]{3,2,1,0:T(2,128)S(1)} %get-tuple-element.8), channel_id=1, replica_groups=mesh['scen'=8,'reach'=64] {'scen'}, dimensions={0} | all-to-all | bytes 81920 | tf_op jit(solution)/shard_map/all_to_all | solution.py:375
  52.9 0.1 shard_map.72
  53.0 17.6 %all_to_all.27.in_ref = f32[64,5,2,128]{3,2,1,0:T(2,128)S(1)} all-to-all(f32[64,5,2,128]{3,2,1,0:T(2,128)S(1)} %shard_map.72), channel_id=1, replica_groups=mesh['scen'=8,'reach'=64] {'reach'}, dimensions={0} | all-to-all | bytes 655360 | tf_op jit(solution)/shard_map/all_to_all | solution.py:375
  70.6 0.1 shard_map.73
  70.7 10.2 %all_to_all.28.gram_ref = f32[8,5,2,128]{3,2,1,0:T(2,128)S(1)} all-to-all(f32[8,5,2,128]{3,2,1,0:T(2,128)S(1)} %shard_map.73), channel_id=1, replica_groups=mesh['scen'=8,'reach'=64] {'scen'}, dimensions={0} | all-to-all | bytes 81920 | tf_op jit(solution)/shard_map/all_to_all | solution.py:375
  81.0 5.8 %shard_map.74 = (f32[2,2048,128]{2,1,0:T(8,128)}, f32[128,128]{1,0:T(8,128)}) custom-call(f32[8,5,2,128]{3,2,1,0:T(2,128)S(1)} %all_to_all.28.gram_ref, bf16[2,128,2048]{2,1,0:T(8,128)(2,1)S(1)} %get-tuple-element.9.cols_ref), custom_call_target="tpu_custom_call" | custom-call | tf_op jit(solution)/shard_map/pallas_call | solution.py:435
Async XLA Ops:
  2.3 27.9 %all-to-all-start = ((f32[64,1,128]{2,1,0:T(1,128)}), f32[64,1,128]{2,1,0:T(1,128)S(1)}, u32[]{:S(2)}, u32[]{:S(2)}) async-start(f32[64,1,128]{2,1,0:T(1,128)} %shard_map.69), calls=%async_computation | async-start | bytes 65536 | tf_op jit(solution)/shard_map/all_to_all | solution.py:375
  20.9 0.9 %copy-start = (f32[1,2,16384]{2,1,0:T(2,128)S(1)}, f32[1,2,16384]{2,1,0:T(2,128)}, u32[]{:S(2)}) copy-start(f32[1,2,16384]{2,1,0:T(2,128)} %param.5) | copy-start | bytes 393220
  21.8 0.8 copy-start.1
